TPU v7x, 32 devices: a whole 2x2x4 slice. The times are simulated.
32 devices in a mesh: section: 4 (over z), pair: 4 (over y, x), dp: 2 (over core).
Axes of the slice: x: 2, y: 2, z: 4, core: 2. Of those that a mesh axis runs over, the one named last changes fastest.
Arguments:
- enc_in: bfloat16 [4, 4096, 768], P(None, ('pair', 'dp')), may hold values from -6 to 6
- dec_in: bfloat16 [4, 8, 768], P(None, ('pair', 'dp')), may hold values from -6 to 6
- lengths: int32 [4, 8], P(None, ('pair', 'dp')), may hold values from 40 to 512, as said below
- weights: bfloat16 [4, 768, 6144], P('section', None, 'pair'), as said below
- gains: float32 [4, 2, 768], P('section'), may hold values from 0.25 to 1.75
- dec_cot: bfloat16 [4, 8, 768], P(None, ('pair', 'dp')), may hold values from -6 to 6
Outputs:
- dec_out: bfloat16 [4, 8, 768], P('section', ('pair', 'dp'))
- enc_grad: bfloat16 [4, 4096, 768], P('section', ('pair', 'dp'))
- dec_grad: bfloat16 [4, 8, 768], P('section', ('pair', 'dp'))
- weight_grad: float32 [4, 768, 6144], P('section', None, 'pair')
- gain_grad: float32 [4, 2, 768], P('section', None, 'pair')
Inputs may be any that keep to these rules, and one draw needn't show every extreme that they name: `lengths`: in every micro-batch one passage, at a place drawn from the seed, has length 512 and another has length 40. `weights`: each section's matrices lie side by side as the steps lay them out.
All inputs are finite; a program needn't handle non-finite values.
Results may differ from a plain program's by a relative error of at most 0.025.
Values may be sent and summed in bfloat16 or wider, within the bound.
A program may use at most 576 MiB of HBM per device.

v0:
```python
import jax
import jax.numpy as jnp
from jax import lax
from jax.sharding import PartitionSpec as P

HEADS = 12
HEAD = 64
FF = 3072
L = 512


EPSILON = 1e-06
NEGATIVE = -1e30


def as_sent(x):

    def short(part):
        return part.astype(jnp.bfloat16) if part.dtype == jnp.float32 else part

    return jax.tree.map(short, x)


def shifted(value, axis, steps):
    count = lax.axis_size(axis)
    initial, last = (max(0, -steps), min(count, count - steps))
    return lax.ppermute(value, axis, [(source, source + steps) for source in range(initial, last)])


def norm_scale(values_in, gain_row):
    return (
        values_in
        * lax.rsqrt(jnp.mean(values_in * values_in, axis=-1, keepdims=True) + EPSILON)
        * gain_row
    )


def norm_back(values_in, gain_row, upstream):
    _, pullback = jax.vjp(norm_scale, values_in, gain_row)
    return pullback(upstream)


def smooth(values_in):
    return jax.nn.gelu(values_in, approximate=True)


def smooth_back(values_in, upstream):
    _, pullback = jax.vjp(smooth, values_in)
    return pullback(upstream)[0]


def matmul(left, right):
    return jnp.dot(left, right, preferred_element_type=jnp.float32)


def matmul_trans(left, right):
    return lax.dot_general(
        left, right, (((1,), (1,)), ((), ())), preferred_element_type=jnp.float32
    )


def outer_sum(left, right):
    return lax.dot_general(
        left, right, (((0,), (0,)), ((), ())), preferred_element_type=jnp.float32
    )


def narrow(values_in):
    return values_in.astype(jnp.bfloat16)


def column_block(weight_cols, index):
    width = weight_cols.shape[0]
    return weight_cols[:, index * width : (index + 1) * width]


def live_keys(lens):
    return lax.broadcasted_iota(jnp.int32, (lens.shape[0], L), 1) < lens[:, None]


def encoder_forward(enc_x, lens, weight_cols, gain_rows):
    seq_count = lens.shape[0]
    head_shape = (seq_count, L, HEADS, HEAD)
    score_scale = HEAD ** (-0.5)
    inputs = enc_x.astype(jnp.float32)
    normed = narrow(norm_scale(inputs, gain_rows[0]))
    queries = narrow(matmul(normed, column_block(weight_cols, 0))).reshape(head_shape)
    key_rows = narrow(matmul(normed, column_block(weight_cols, 1))).reshape(head_shape)
    value_rows = narrow(matmul(normed, column_block(weight_cols, 2))).reshape(head_shape)
    scores = (
        jnp.einsum("bqhd,bkhd->bhqk", queries, key_rows, preferred_element_type=jnp.float32)
        * score_scale
    )
    scores = jnp.where(live_keys(lens)[:, None, None, :], scores, NEGATIVE)
    soft_probs = jax.nn.softmax(scores, axis=-1)
    mixed = jnp.einsum(
        "bhqk,bkhd->bqhd", narrow(soft_probs), value_rows, preferred_element_type=jnp.float32
    )
    attended = narrow(mixed).reshape(seq_count * L, HEADS * HEAD)
    result = narrow(inputs + matmul_trans(attended, column_block(weight_cols, 3)))
    return (result, (inputs, normed, queries, key_rows, value_rows, soft_probs, attended))


def encoder_backward(enc_x, dec_x, lens, weight_cols, gain_rows, grad_enc, grad_dec):
    _, kept = encoder_forward(enc_x, lens, weight_cols, gain_rows)
    inputs, normed, queries, key_rows, value_rows, soft_probs, attended = kept
    seq_count = lens.shape[0]
    head_shape = (seq_count, L, HEADS, HEAD)
    flat_shape = (seq_count * L, HEADS * HEAD)
    score_scale = HEAD ** (-0.5)
    grad_out_proj = outer_sum(grad_enc, attended)
    grad_attended = narrow(matmul(grad_enc, column_block(weight_cols, 3))).reshape(head_shape)
    grad_values = narrow(
        jnp.einsum(
            "bhqk,bqhd->bkhd", narrow(soft_probs), grad_attended, preferred_element_type=jnp.float32
        )
    )
    grad_probs = jnp.einsum(
        "bqhd,bkhd->bhqk", grad_attended, value_rows, preferred_element_type=jnp.float32
    )
    grad_scores = narrow(
        soft_probs * (grad_probs - jnp.sum(grad_probs * soft_probs, axis=-1, keepdims=True))
    )
    grad_queries = narrow(
        jnp.einsum("bhqk,bkhd->bqhd", grad_scores, key_rows, preferred_element_type=jnp.float32)
        * score_scale
    ).reshape(flat_shape)
    grad_keys = narrow(
        jnp.einsum("bhqk,bqhd->bkhd", grad_scores, queries, preferred_element_type=jnp.float32)
        * score_scale
    ).reshape(flat_shape)
    grad_values = grad_values.reshape(flat_shape)
    grad_normed = (
        matmul_trans(grad_queries, column_block(weight_cols, 0))
        + matmul_trans(grad_keys, column_block(weight_cols, 1))
        + matmul_trans(grad_values, column_block(weight_cols, 2))
    )
    grad_inputs, grad_gain = norm_back(inputs, gain_rows[0], grad_normed)
    grad_in = narrow(grad_enc.astype(jnp.float32) + grad_inputs)
    width = weight_cols.shape[0]
    weight_grad = jnp.concatenate(
        [
            outer_sum(normed, grad_queries),
            outer_sum(normed, grad_keys),
            outer_sum(normed, grad_values),
            grad_out_proj,
            jnp.zeros((width, weight_cols.shape[1] - 4 * width), jnp.float32),
        ],
        axis=1,
    )
    gain_grad = jnp.stack([grad_gain, jnp.zeros_like(grad_gain)])
    return (grad_in, jnp.zeros_like(grad_dec), weight_grad, gain_grad)


def feed_forward(rows_in, weight_cols, gain_rows):
    inputs = rows_in.astype(jnp.float32)
    normed = narrow(norm_scale(inputs, gain_rows[0]))
    hidden = matmul(normed, weight_cols[:, :FF])
    activated = narrow(smooth(hidden))
    middle = inputs + matmul_trans(activated, weight_cols[:, FF:])
    result = narrow(norm_scale(middle, gain_rows[1]))
    return (result, (inputs, normed, hidden, activated, middle))


def feed_backward(rows_in, weight_cols, gain_rows, upstream):
    _, kept = feed_forward(rows_in, weight_cols, gain_rows)
    inputs, normed, hidden, activated, middle = kept
    grad_middle, grad_final_gain = norm_back(middle, gain_rows[1], upstream.astype(jnp.float32))
    grad_branch = narrow(grad_middle)
    grad_down = outer_sum(grad_branch, activated)
    grad_hidden = narrow(smooth_back(hidden, matmul(grad_branch, weight_cols[:, FF:])))
    grad_up = outer_sum(normed, grad_hidden)
    grad_inputs, grad_first_gain = norm_back(
        inputs, gain_rows[0], matmul_trans(grad_hidden, weight_cols[:, :FF])
    )
    grad_in = narrow(grad_middle + grad_inputs)
    return (
        grad_in,
        jnp.concatenate([grad_up, grad_down], axis=1),
        jnp.stack([grad_first_gain, grad_final_gain]),
    )


def decoder_forward(enc_x, dec_x, lens, weight_cols, gain_rows):
    seq_count = lens.shape[0]
    head_shape = (seq_count, L, HEADS, HEAD)
    score_scale = HEAD ** (-0.5)
    inputs = dec_x.astype(jnp.float32)
    normed_self = narrow(norm_scale(inputs, gain_rows[0]))
    self_values = narrow(matmul(normed_self, column_block(weight_cols, 0)))
    middle = inputs + matmul_trans(self_values, column_block(weight_cols, 1))
    normed_cross = narrow(norm_scale(middle, gain_rows[1]))
    queries = narrow(matmul(normed_cross, column_block(weight_cols, 2))).reshape(
        seq_count, HEADS, HEAD
    )
    key_rows = narrow(matmul(enc_x, column_block(weight_cols, 3))).reshape(head_shape)
    value_rows = narrow(matmul(enc_x, column_block(weight_cols, 4))).reshape(head_shape)
    scores = (
        jnp.einsum("bhd,bkhd->bhk", queries, key_rows, preferred_element_type=jnp.float32)
        * score_scale
    )
    scores = jnp.where(live_keys(lens)[:, None, :], scores, NEGATIVE)
    soft_probs = jax.nn.softmax(scores, axis=-1)
    mixed = jnp.einsum(
        "bhk,bkhd->bhd", narrow(soft_probs), value_rows, preferred_element_type=jnp.float32
    )
    attended = narrow(mixed).reshape(seq_count, HEADS * HEAD)
    result = narrow(middle + matmul_trans(attended, column_block(weight_cols, 5)))
    return (
        result,
        (
            inputs,
            normed_self,
            self_values,
            middle,
            normed_cross,
            queries,
            key_rows,
            value_rows,
            soft_probs,
            attended,
        ),
    )


def decoder_backward(enc_x, dec_x, lens, weight_cols, gain_rows, grad_enc, grad_dec):
    _, kept = decoder_forward(enc_x, dec_x, lens, weight_cols, gain_rows)
    (
        inputs,
        normed_self,
        self_values,
        middle,
        normed_cross,
        queries,
        key_rows,
        value_rows,
        soft_probs,
        attended,
    ) = kept
    seq_count = lens.shape[0]
    flat_shape = (seq_count * L, HEADS * HEAD)
    score_scale = HEAD ** (-0.5)
    grad_cross_out = outer_sum(grad_dec, attended)
    grad_attended = narrow(matmul(grad_dec, column_block(weight_cols, 5))).reshape(
        seq_count, HEADS, HEAD
    )
    grad_values = narrow(
        jnp.einsum(
            "bhk,bhd->bkhd", narrow(soft_probs), grad_attended, preferred_element_type=jnp.float32
        )
    ).reshape(flat_shape)
    grad_probs = jnp.einsum(
        "bhd,bkhd->bhk", grad_attended, value_rows, preferred_element_type=jnp.float32
    )
    grad_scores = narrow(
        soft_probs * (grad_probs - jnp.sum(grad_probs * soft_probs, axis=-1, keepdims=True))
    )
    grad_queries = narrow(
        jnp.einsum("bhk,bkhd->bhd", grad_scores, key_rows, preferred_element_type=jnp.float32)
        * score_scale
    ).reshape(seq_count, HEADS * HEAD)
    grad_keys = narrow(
        jnp.einsum("bhk,bhd->bkhd", grad_scores, queries, preferred_element_type=jnp.float32)
        * score_scale
    ).reshape(flat_shape)
    grad_encoded = narrow(
        matmul_trans(grad_keys, column_block(weight_cols, 3))
        + matmul_trans(grad_values, column_block(weight_cols, 4))
    )
    grad_middle_part, grad_cross_gain = norm_back(
        middle, gain_rows[1], matmul_trans(grad_queries, column_block(weight_cols, 2))
    )
    grad_middle = grad_dec.astype(jnp.float32) + grad_middle_part
    grad_branch = narrow(grad_middle)
    grad_self_out = outer_sum(grad_branch, self_values)
    grad_self_values = narrow(matmul(grad_branch, column_block(weight_cols, 1)))
    grad_inputs, grad_self_gain = norm_back(
        inputs, gain_rows[0], matmul_trans(grad_self_values, column_block(weight_cols, 0))
    )
    grad_dec_in = narrow(grad_middle + grad_inputs)
    width = weight_cols.shape[0]
    weight_grad = jnp.concatenate(
        [
            outer_sum(normed_self, grad_self_values),
            grad_self_out,
            outer_sum(normed_cross, grad_queries),
            outer_sum(enc_x, grad_keys),
            outer_sum(enc_x, grad_values),
            grad_cross_out,
            jnp.zeros((width, weight_cols.shape[1] - 6 * width), jnp.float32),
        ],
        axis=1,
    )
    gain_grad = jnp.stack([grad_self_gain, grad_cross_gain])
    return (grad_encoded, grad_dec_in, weight_grad, gain_grad)


def attend_step(enc_x, dec_x, lens, weight_cols, gain_rows):
    return (encoder_forward(enc_x, lens, weight_cols, gain_rows)[0], jnp.zeros_like(dec_x))


def encode_step(enc_x, dec_x, lens, weight_cols, gain_rows):
    return (feed_forward(enc_x, weight_cols, gain_rows)[0], jnp.zeros_like(dec_x))


def cross_step(enc_x, dec_x, lens, weight_cols, gain_rows):
    return (jnp.zeros_like(enc_x), decoder_forward(enc_x, dec_x, lens, weight_cols, gain_rows)[0])


def final_step(enc_x, dec_x, lens, weight_cols, gain_rows):
    return (jnp.zeros_like(enc_x), feed_forward(dec_x, weight_cols, gain_rows)[0])


def resting_step(enc_x, dec_x, lens, weight_cols, gain_rows):
    return (jnp.zeros_like(enc_x), jnp.zeros_like(dec_x))


def encode_back(enc_x, dec_x, lens, weight_cols, gain_rows, grad_enc, grad_dec):
    grad_in, weight_grad, gain_grad = feed_backward(enc_x, weight_cols, gain_rows, grad_enc)
    return (grad_in, jnp.zeros_like(dec_x), weight_grad, gain_grad)


def final_back(enc_x, dec_x, lens, weight_cols, gain_rows, grad_enc, grad_dec):
    grad_in, weight_grad, gain_grad = feed_backward(dec_x, weight_cols, gain_rows, grad_dec)
    return (jnp.zeros_like(enc_x), grad_in, weight_grad, gain_grad)


def resting_back(enc_x, dec_x, lens, weight_cols, gain_rows, grad_enc, grad_dec):
    return (
        jnp.zeros_like(enc_x),
        jnp.zeros_like(dec_x),
        jnp.zeros(weight_cols.shape, jnp.float32),
        jnp.zeros_like(gain_rows),
    )


def body(enc_in, dec_in, lengths, weights, gains, dec_cot):
    sections = lax.axis_size("section")
    section_idx = lax.axis_index("section")
    mb_count = enc_in.shape[0]
    rows = enc_in.shape[1]
    seq_count = dec_in.shape[1]
    width = enc_in.shape[2]
    weight_cols = lax.all_gather(weights[0], "pair", axis=1, tiled=True)
    gain_rows = gains[0]
    forward_table = [attend_step, encode_step, cross_step, final_step, resting_step]
    backward_table = [encoder_backward, encode_back, decoder_backward, final_back, resting_back]
    ticks = mb_count + sections - 1
    carry = jnp.zeros((rows + seq_count, width), jnp.bfloat16)
    stash = jnp.zeros((mb_count, rows + seq_count, width), jnp.bfloat16)
    outputs_all = jnp.zeros((mb_count, seq_count, width), jnp.bfloat16)
    for tick_num in range(ticks):
        micro = tick_num - section_idx
        valid = (micro >= 0) & (micro < mb_count)
        slot = jnp.clip(micro, 0, mb_count - 1)
        enc_x = jnp.where(section_idx == 0, enc_in[slot], carry[:rows])
        dec_x = jnp.where(section_idx == 2, dec_in[slot], carry[rows:])
        branch = jnp.where(valid, section_idx, sections)
        enc_y, dec_y = lax.switch(
            branch, forward_table, enc_x, dec_x, lengths[slot], weight_cols, gain_rows
        )
        stash = stash.at[slot].set(
            jnp.where(valid, jnp.concatenate([enc_x, dec_x], axis=0), stash[slot])
        )
        outputs_all = outputs_all.at[slot].set(
            jnp.where(valid & (section_idx == sections - 1), dec_y, outputs_all[slot])
        )
        if tick_num + 1 < ticks:
            carry = shifted(as_sent(jnp.concatenate([enc_y, dec_y], axis=0)), "section", 1)
    grads_weight = jnp.zeros(weight_cols.shape, jnp.float32)
    grads_gain = jnp.zeros(gain_rows.shape, jnp.float32)
    enc_grads = jnp.zeros((mb_count, rows, width), jnp.bfloat16)
    dec_grads = jnp.zeros((mb_count, seq_count, width), jnp.bfloat16)
    carry = jnp.zeros((rows + seq_count, width), jnp.bfloat16)
    for tick_num in range(ticks):
        micro = tick_num - (sections - 1 - section_idx)
        valid = (micro >= 0) & (micro < mb_count)
        slot = jnp.clip(micro, 0, mb_count - 1)
        saved = stash[slot]
        grad_enc = carry[:rows]
        grad_dec = jnp.where(section_idx == sections - 1, dec_cot[slot], carry[rows:])
        branch = jnp.where(valid, section_idx, sections)
        enc_back, dec_back, weight_part, gain_part = lax.switch(
            branch,
            backward_table,
            saved[:rows],
            saved[rows:],
            lengths[slot],
            weight_cols,
            gain_rows,
            grad_enc,
            grad_dec,
        )
        grads_weight = grads_weight + weight_part
        grads_gain = grads_gain + gain_part
        enc_grads = enc_grads.at[slot].set(
            jnp.where(valid & (section_idx == 0), enc_back, enc_grads[slot])
        )
        dec_grads = dec_grads.at[slot].set(
            jnp.where(valid & (section_idx == 2), dec_back, dec_grads[slot])
        )
        if tick_num + 1 < ticks:
            carry = shifted(as_sent(jnp.concatenate([enc_back, dec_back], axis=0)), "section", -1)
    own_out, own_enc, own_dec = (
        lax.all_to_all(outputs_all, "section", split_axis=0, concat_axis=0, tiled=True),
        lax.all_to_all(enc_grads, "section", split_axis=0, concat_axis=0, tiled=True),
        lax.all_to_all(dec_grads, "section", split_axis=0, concat_axis=0, tiled=True),
    )
    share_weight, share_gain = (
        lax.psum_scatter(
            grads_weight.astype(jnp.bfloat16), "pair", scatter_dimension=1, tiled=True
        ).astype(jnp.float32),
        lax.psum_scatter(
            grads_gain.astype(jnp.bfloat16), "pair", scatter_dimension=1, tiled=True
        ).astype(jnp.float32),
    )
    total_weight, total_gain = (
        lax.psum(share_weight.astype(jnp.bfloat16), "dp").astype(jnp.float32),
        lax.psum(share_gain.astype(jnp.bfloat16), "dp").astype(jnp.float32),
    )
    return (
        own_out[sections - 1][None],
        own_enc[0][None],
        own_dec[2][None],
        total_weight[None],
        total_gain[None],
    )


def solution(mesh):
    return jax.shard_map(
        body,
        mesh=mesh,
        in_specs=(
            P(None, ("pair", "dp"), None),
            P(None, ("pair", "dp"), None),
            P(None, ("pair", "dp")),
            P("section", None, "pair"),
            P("section", None, None),
            P(None, ("pair", "dp"), None),
        ),
        out_specs=(
            P("section", ("pair", "dp"), None),
            P("section", ("pair", "dp"), None),
            P("section", ("pair", "dp"), None),
            P("section", None, "pair"),
            P("section", None, "pair"),
        ),
        check_vma=False,
    )
```

profile of v0, /device:TPU:0, one launch (start us, length us, event | category | flops | bytes accessed | tf_op | source)
XLA Modules:
  0.0 1312.4 jit_solution(5627478082551830262)
XLA Ops:
  11.8 97.2 %all-gather.3.cloned.1.call-done = bf16[1,768,6144]{2,1,0:T(8,128)(2,1)} async-done(((bf16[1,768,1536]{2,1,0:T(8,128)(2,1)}), bf16[1,768,6144]{2,1,0:T(8,128)(2,1)}) %all-gather.3.cloned.1.call-update) | async-done | bytes 9437200 | tf_op jit(solution)/shard_map/all_gather | solution.py:344
  108.9 34.3 %conditional.14 = (bf16[512,768]{1,0:T(8,128)(2,1)S(1)}, bf16[1,768]{1,0:T(2,128)(2,1)S(1)}) conditional(s32[]{:T(128)} %clamp.42, (bf16[512,768]{1,0:T(8,128)(2,1)S(1)}, f32[2,768]{1,0:T(2,128)S(1)}, bf16[768,6144]{1,0:T(8,128)(2,1)}, s32[1,1]{1,0:T(1,128)}) %tuple.857, (bf16[512,768]{1,0:T(8,128)(2,1)S(1)}, ...), branch_computations={%region_1.0_spmd, %region_5.8_spmd, %region_8.0_spmd, %region_13.1... | conditional | flops 4851500032 | bytes 45692440 | solution.py:359
  119.1 7.5 fusion.1889
  144.7 17.3 %collective-permute-done = bf16[513,768]{1,0:T(8,128)(2,1)S(1)} collective-permute-done((bf16[513,768]{1,0:T(8,128)(2,1)S(1)}, bf16[513,768]{1,0:T(8,128)(2,1)S(1)}, u32[]{:S(2)}, u32[]{:S(2)}) %collective-permute-start) | collective-permute-done | bytes 788000 | tf_op jit(solution)/shard_map/ppermute | solution.py:27
  164.7 34.5 %conditional.15 = (bf16[512,768]{1,0:T(8,128)(2,1)S(1)}, bf16[1,768]{1,0:T(2,128)(2,1)S(1)}) conditional(s32[]{:T(128)} %clamp.43, (bf16[512,768]{1,0:T(8,128)(2,1)}, f32[2,768]{1,0:T(2,128)S(1)}, bf16[768,6144]{1,0:T(8,128)(2,1)}, s32[1,1]{1,0:T(1,128)}) %tuple.861, (bf16[512,768]{1,0:T(8,128)(2,1)}, ...), branch_computations={%region_18.22_spmd, %region_22.25_spmd, %region_25.30_spmd, %regio... | conditional | flops 4851500032 | bytes 45692440 | solution.py:359
  174.6 7.5 fusion.1890
  200.6 16.7 %collective-permute-done.1 = bf16[513,768]{1,0:T(8,128)(2,1)S(1)} collective-permute-done((bf16[513,768]{1,0:T(8,128)(2,1)S(1)}, bf16[513,768]{1,0:T(8,128)(2,1)S(1)}, u32[]{:S(2)}, u32[]{:S(2)}) %collective-permute-start.1) | collective-permute-done | bytes 788000 | tf_op jit(solution)/shard_map/ppermute | solution.py:27
  218.5 34.3 %conditional.16 = (bf16[512,768]{1,0:T(8,128)(2,1)S(1)}, bf16[1,768]{1,0:T(2,128)(2,1)S(1)}) conditional(s32[]{:T(128)} %clamp.44, (bf16[512,768]{1,0:T(8,128)(2,1)S(1)}, f32[2,768]{1,0:T(2,128)S(1)}, bf16[768,6144]{1,0:T(8,128)(2,1)}, s32[1,1]{1,0:T(1,128)}) %tuple.868, (bf16[512,768]{1,0:T(8,128)(2,1)S(1)}, ...), branch_computations={%region_35.39_spmd, %region_39.42_spmd, %region_42.47_spmd, %regio... | conditional | flops 4851500032 | bytes 45692440 | solution.py:359
  228.7 7.5 fusion.1891
  254.2 16.1 %collective-permute-done.2 = bf16[513,768]{1,0:T(8,128)(2,1)S(1)} collective-permute-done((bf16[513,768]{1,0:T(8,128)(2,1)S(1)}, bf16[513,768]{1,0:T(8,128)(2,1)S(1)}, u32[]{:S(2)}, u32[]{:S(2)}) %collective-permute-start.2) | collective-permute-done | bytes 788000 | tf_op jit(solution)/shard_map/ppermute | solution.py:27
  271.6 33.3 %conditional.17 = (bf16[512,768]{1,0:T(8,128)(2,1)S(1)}, bf16[1,768]{1,0:T(2,128)(2,1)S(1)}) conditional(s32[]{:T(128)} %clamp.45, (bf16[512,768]{1,0:T(8,128)(2,1)S(1)}, f32[2,768]{1,0:T(2,128)S(1)}, bf16[768,6144]{1,0:T(8,128)(2,1)}, s32[1,1]{1,0:T(1,128)}) %tuple.869, (bf16[512,768]{1,0:T(8,128)(2,1)S(1)}, ...), branch_computations={%region_52.56_spmd, %region_56.59_spmd, %region_59.64_spmd, %regio... | conditional | flops 4851500032 | bytes 45692440 | solution.py:359
  284.7 7.4 fusion.1892
  306.3 15.5 %collective-permute-done.3 = bf16[513,768]{1,0:T(8,128)(2,1)S(1)} collective-permute-done((bf16[513,768]{1,0:T(8,128)(2,1)S(1)}, bf16[513,768]{1,0:T(8,128)(2,1)S(1)}, u32[]{:S(2)}, u32[]{:S(2)}) %collective-permute-start.3) | collective-permute-done | bytes 788000 | tf_op jit(solution)/shard_map/ppermute | solution.py:27
  327.7 17.9 %collective-permute-start.4 = (bf16[513,768]{1,0:T(8,128)(2,1)S(1)}, bf16[513,768]{1,0:T(8,128)(2,1)}, u32[]{:S(2)}, u32[]{:S(2)}) collective-permute-start(bf16[513,768]{1,0:T(8,128)(2,1)S(1)} %pad_maximum_fusion.39), channel_id=1, source_target_pairs={{0,8},{8,16},{16,24},{1,9},{9,17},{17,25},{2,10},{10,18},{18,26},{... | collective-permute-start | bytes 2363912 | tf_op jit(solution)/shard_map/ppermute | solution.py:27
  350.0 9.3 collective-permute-done.4
  392.2 22.0 %conditional.21 = (bf16[512,768]{1,0:T(8,128)(2,1)}, bf16[1,768]{1,0:T(2,128)(2,1)S(1)}, f32[768,6144]{1,0:T(8,128)}, f32[2,768]{1,0:T(2,128)S(1)}) conditional(s32[]{:T(128)} %clamp.49, (bf16[512,768]{1,0:T(8,128)(2,1)S(1)}, f32[2,768]{1,0:T(2,128)S(1)}, bf16[768,6144]{1,0:T(8,128)(2,1)}, ...), branch_computations={%region_115.122_spmd, %region_122.0_spmd, %region_129.137_spmd, %r... | conditional | flops 14579277824 | bytes 229501536 | solution.py:383
  405.2 8.8 broadcast.2930
  416.8 38.6 %collective-permute-done.6 = bf16[513,768]{1,0:T(8,128)(2,1)S(1)} collective-permute-done((bf16[513,768]{1,0:T(8,128)(2,1)S(1)}, bf16[513,768]{1,0:T(8,128)(2,1)S(1)}, u32[]{:S(2)}, u32[]{:S(2)}) %collective-permute-start.6) | collective-permute-done | bytes 788000 | tf_op jit(solution)/shard_map/ppermute | solution.py:27
  455.5 21.9 %conditional.22 = (bf16[512,768]{1,0:T(8,128)(2,1)}, bf16[1,768]{1,0:T(2,128)(2,1)S(1)}, f32[768,6144]{1,0:T(8,128)}, f32[2,768]{1,0:T(2,128)S(1)}) conditional(s32[]{:T(128)} %clamp.50, (bf16[512,768]{1,0:T(8,128)(2,1)S(1)}, bf16[512,768]{1,0:T(8,128)(2,1)S(1)}, f32[2,768]{1,0:T(2,128)S(1)}, ...), branch_computations={%region_144.0_spmd, %region_151.0_spmd, %region_158.166_spmd, %reg... | conditional | flops 14582421504 | bytes 257026752 | solution.py:383
  468.4 8.8 broadcast.2962
  480.1 16.3 %collective-permute-done.7 = bf16[513,768]{1,0:T(8,128)(2,1)S(1)} collective-permute-done((bf16[513,768]{1,0:T(8,128)(2,1)S(1)}, bf16[513,768]{1,0:T(8,128)(2,1)S(1)}, u32[]{:S(2)}, u32[]{:S(2)}) %collective-permute-start.7) | collective-permute-done | bytes 788000 | tf_op jit(solution)/shard_map/ppermute | solution.py:27
  496.5 22.0 %conditional.23 = (bf16[512,768]{1,0:T(8,128)(2,1)}, bf16[1,768]{1,0:T(2,128)(2,1)S(1)}, f32[768,6144]{1,0:T(8,128)}, f32[2,768]{1,0:T(2,128)S(1)}) conditional(s32[]{:T(128)} %clamp.51, (bf16[512,768]{1,0:T(8,128)(2,1)S(1)}, bf16[512,768]{1,0:T(8,128)(2,1)S(1)}, f32[2,768]{1,0:T(2,128)S(1)}, ...), branch_computations={%region_173.0_spmd, %region_180.187_spmd, %region_187.195_spmd, %r... | conditional | flops 14582421504 | bytes 257026752 | solution.py:383
  509.5 8.7 broadcast.2994
  521.2 125.0 %collective-permute-done.8 = bf16[513,768]{1,0:T(8,128)(2,1)S(1)} collective-permute-done((bf16[513,768]{1,0:T(8,128)(2,1)S(1)}, bf16[513,768]{1,0:T(8,128)(2,1)S(1)}, u32[]{:S(2)}, u32[]{:S(2)}) %collective-permute-start.8) | collective-permute-done | bytes 788000 | tf_op jit(solution)/shard_map/ppermute | solution.py:27
  646.3 104.4 %conditional.24 = (bf16[512,768]{1,0:T(8,128)(2,1)}, bf16[1,768]{1,0:T(2,128)(2,1)S(1)}, f32[768,6144]{1,0:T(8,128)}, f32[2,768]{1,0:T(2,128)S(1)}) conditional(s32[]{:T(128)} %clamp.52, (bf16[512,768]{1,0:T(8,128)(2,1)S(1)}, bf16[512,768]{1,0:T(8,128)(2,1)S(1)}, f32[2,768]{1,0:T(2,128)S(1)}, ...), branch_computations={%region_202.0_spmd, %region_209.0_spmd, %region_216.0_spmd, %regio... | conditional | flops 14582421504 | bytes 257026752 | solution.py:383
  662.9 7.4 fusion.1898
  670.3 7.0 fusion.1196
  685.3 6.9 multiply_reduce_fusion.67
  753.4 14.5 %collective-permute-done.9 = bf16[513,768]{1,0:T(8,128)(2,1)S(1)} collective-permute-done((bf16[513,768]{1,0:T(8,128)(2,1)S(1)}, bf16[513,768]{1,0:T(8,128)(2,1)S(1)}, u32[]{:S(2)}, u32[]{:S(2)}) %collective-permute-start.9) | collective-permute-done | bytes 788000 | tf_op jit(solution)/shard_map/ppermute | solution.py:27
  768.0 104.5 %conditional.25 = (bf16[512,768]{1,0:T(8,128)(2,1)}, bf16[1,768]{1,0:T(2,128)(2,1)S(1)}, f32[768,6144]{1,0:T(8,128)}, f32[2,768]{1,0:T(2,128)S(1)}) conditional(s32[]{:T(128)} %clamp.53, (bf16[512,768]{1,0:T(8,128)(2,1)S(1)}, bf16[512,768]{1,0:T(8,128)(2,1)S(1)}, f32[2,768]{1,0:T(2,128)S(1)}, ...), branch_computations={%region_231.0_spmd, %region_238.0_spmd, %region_245.253_spmd, %reg... | conditional | flops 14582421504 | bytes 257026752 | solution.py:383
  784.6 7.4 fusion.1899
  792.0 7.0 fusion.1347
  807.1 6.9 multiply_reduce_fusion.77
  875.2 13.6 %collective-permute-done.10 = bf16[513,768]{1,0:T(8,128)(2,1)S(1)} collective-permute-done((bf16[513,768]{1,0:T(8,128)(2,1)S(1)}, bf16[513,768]{1,0:T(8,128)(2,1)S(1)}, u32[]{:S(2)}, u32[]{:S(2)}) %collective-permute-start.10) | collective-permute-done | bytes 788000 | tf_op jit(solution)/shard_map/ppermute | solution.py:27
  889.0 104.5 %conditional.26 = (bf16[512,768]{1,0:T(8,128)(2,1)}, bf16[1,768]{1,0:T(2,128)(2,1)S(1)}, f32[768,6144]{1,0:T(8,128)}, f32[2,768]{1,0:T(2,128)S(1)}) conditional(s32[]{:T(128)} %clamp.54, (bf16[512,768]{1,0:T(8,128)(2,1)S(1)}, bf16[512,768]{1,0:T(8,128)(2,1)S(1)}, f32[2,768]{1,0:T(2,128)S(1)}, ...), branch_computations={%region_260.0_spmd, %region_267.274_spmd, %region_274.282_spmd, %r... | conditional | flops 14582421504 | bytes 257026752 | solution.py:383
  905.5 7.4 fusion.1900
  912.9 7.0 fusion.1498
  927.9 6.9 multiply_reduce_fusion.87
  996.1 12.7 collective-permute-done.11
  1008.9 103.6 %conditional.27 = (bf16[512,768]{1,0:T(8,128)(2,1)}, bf16[1,768]{1,0:T(2,128)(2,1)S(1)}, f32[768,6144]{1,0:T(8,128)}, f32[2,768]{1,0:T(2,128)S(1)}) conditional(s32[]{:T(128)} %clamp.55, (bf16[512,768]{1,0:T(8,128)(2,1)S(1)}, bf16[512,768]{1,0:T(8,128)(2,1)S(1)}, f32[2,768]{1,0:T(2,128)S(1)}, ...), branch_computations={%region_289.0_spmd, %region_296.0_spmd, %region_303.311_spmd, %reg... | conditional | flops 14582421504 | bytes 257026752 | solution.py:383
  1025.6 7.4 fusion.1901
  1033.0 7.0 fusion.1649
  1048.1 6.9 multiply_reduce_fusion.97
  1112.6 44.5 %add_convert_fusion.7 = bf16[768,6144]{1,0:T(8,128)(2,1)} fusion(f32[768,6144]{1,0:T(8,128)} %get-tuple-element.1123, f32[768,6144]{1,0:T(8,128)} %get-tuple-element.1122, f32[768,6144]{1,0:T(8,128)} %get-tuple-element.1121, f32[768,6144]{1,0:T(8,128)} %get-tuple-element.1120, f32[768,6144]{1,0:T(8,128)} %get-tuple-element.1119, ...), kind=kLoop, calls=%fused_computation.2482 | loop fusion | flops 33030144 | bytes 141557760 | tf_op jit(solution)/shard_map/convert_element_type | solution.py:411
  1201.5 10.4 all-to-all-done.2
  1216.6 33.1 %reduce-scatter.5.cloned.1.call-done = bf16[768,1536]{1,0:T(8,128)(2,1)} async-done(((bf16[768,6144]{1,0:T(8,128)(2,1)}), bf16[768,1536]{1,0:T(8,128)(2,1)}) %reduce-scatter.5.cloned.1.call-update) | async-done | bytes 2359312 | tf_op jit(solution)/shard_map/reduce_scatter | solution.py:410
  1250.3 26.8 %reduce-scatter.7.cloned.1.call-done = bf16[192,2]{1,0:T(8,128)(2,1)} async-done(((bf16[768,2]{1,0:T(8,128)(2,1)}), bf16[192,2]{1,0:T(8,128)(2,1)}) %reduce-scatter.7.cloned.1.call-update) | async-done | bytes 784
  1282.5 18.4 %all-reduce.9.cloned.1.call-done = bf16[1,768,1536]{2,1,0:T(8,128)(2,1)} async-done(((bf16[1,768,1536]{2,1,0:T(8,128)(2,1)}), bf16[1,768,1536]{2,1,0:T(8,128)(2,1)}) %all-reduce.9.cloned.1.call-update) | async-done | bytes 2359312 | tf_op jit(solution)/shard_map/psum | solution.py:418
  (520 shorter events, 434.6 us)
Async XLA Ops:
  7.2 101.8 %copy-start.6 = (f32[1,2,768]{2,1,0:T(2,128)S(1)}, f32[1,2,768]{2,1,0:T(2,128)}, u32[]{:S(2)}) copy-start(f32[1,2,768]{2,1,0:T(2,128)} %param.136) | copy-start | bytes 18436
  7.2 101.7 %all-gather.3.cloned.1.call-start = ((), (), s32[]{:S(2)}) async-start(), calls=%async_computation.7 | async-start | bytes 11796480 | tf_op jit(solution)/shard_map/all_gather | solution.py:344
  7.9 1241.8 %reduce-scatter.5.cloned.1.call-start = ((), (), s32[]{:S(2)}) async-start(), calls=%async_computation.5 | async-start | bytes 11796480 | tf_op jit(solution)/shard_map/reduce_scatter | solution.py:410
  143.3 20.8 %copy-start.94 = (bf16[1,768]{1,0:T(2,128)(2,1)}, bf16[1,768]{1,0:T(2,128)(2,1)S(1)}, u32[]{:S(2)}) copy-start(bf16[1,768]{1,0:T(2,128)(2,1)S(1)} %get-tuple-element.1091) | copy-start | bytes 4612
  143.3 20.8 %copy-start.73 = (bf16[4,1,768]{2,0,1:T(4,128)(2,1)S(1)}, bf16[4,1,768]{2,0,1:T(4,128)(2,1)}, u32[]{:S(2)}) copy-start(bf16[4,1,768]{2,0,1:T(4,128)(2,1)} %param.133) | copy-start | bytes 18436
  143.3 18.6 %collective-permute-start = (bf16[513,768]{1,0:T(8,128)(2,1)S(1)}, bf16[513,768]{1,0:T(8,128)(2,1)S(1)}, u32[]{:S(2)}, u32[]{:S(2)}) collective-permute-start(bf16[513,768]{1,0:T(8,128)(2,1)S(1)} %pad_maximum_fusion.35), channel_id=1, source_target_pairs={{0,8},{8,16},{16,24},{1,9},{9,17},{17,25},{2,10},{10,18},{18,26},{... | collective-permute-start | bytes 2363912 | tf_op jit(solution)/shard_map/ppermute | solution.py:27
  199.1 19.4 %copy-start.96 = (bf16[1,768]{1,0:T(2,128)(2,1)}, bf16[1,768]{1,0:T(2,128)(2,1)S(1)}, u32[]{:S(2)}) copy-start(bf16[1,768]{1,0:T(2,128)(2,1)S(1)} %get-tuple-element.1093) | copy-start | bytes 4612
  199.2 18.1 %collective-permute-start.1 = (bf16[513,768]{1,0:T(8,128)(2,1)S(1)}, bf16[513,768]{1,0:T(8,128)(2,1)S(1)}, u32[]{:S(2)}, u32[]{:S(2)}) collective-permute-start(bf16[513,768]{1,0:T(8,128)(2,1)S(1)} %pad_maximum_fusion.36), channel_id=1, source_target_pairs={{0,8},{8,16},{16,24},{1,9},{9,17},{17,25},{2,10},{10,18},{18,26},{... | collective-permute-start | bytes 2363912 | tf_op jit(solution)/shard_map/ppermute | solution.py:27
  252.8 18.8 %copy-start.98 = (bf16[1,768]{1,0:T(2,128)(2,1)}, bf16[1,768]{1,0:T(2,128)(2,1)S(1)}, u32[]{:S(2)}) copy-start(bf16[1,768]{1,0:T(2,128)(2,1)S(1)} %get-tuple-element.1095) | copy-start | bytes 4612
  252.9 17.5 %collective-permute-start.2 = (bf16[513,768]{1,0:T(8,128)(2,1)S(1)}, bf16[513,768]{1,0:T(8,128)(2,1)S(1)}, u32[]{:S(2)}, u32[]{:S(2)}) collective-permute-start(bf16[513,768]{1,0:T(8,128)(2,1)S(1)} %pad_maximum_fusion.37), channel_id=1, source_target_pairs={{0,8},{8,16},{16,24},{1,9},{9,17},{17,25},{2,10},{10,18},{18,26},{... | collective-permute-start | bytes 2363912 | tf_op jit(solution)/shard_map/ppermute | solution.py:27
  304.9 18.1 %copy-start.100 = (bf16[1,768]{1,0:T(2,128)(2,1)}, bf16[1,768]{1,0:T(2,128)(2,1)S(1)}, u32[]{:S(2)}) copy-start(bf16[1,768]{1,0:T(2,128)(2,1)S(1)} %get-tuple-element.1097) | copy-start | bytes 4612
  305.0 16.8 %collective-permute-start.3 = (bf16[513,768]{1,0:T(8,128)(2,1)S(1)}, bf16[513,768]{1,0:T(8,128)(2,1)S(1)}, u32[]{:S(2)}, u32[]{:S(2)}) collective-permute-start(bf16[513,768]{1,0:T(8,128)(2,1)S(1)} %pad_maximum_fusion.38), channel_id=1, source_target_pairs={{0,8},{8,16},{16,24},{1,9},{9,17},{17,25},{2,10},{10,18},{18,26},{... | collective-permute-start | bytes 2363912 | tf_op jit(solution)/shard_map/ppermute | solution.py:27
  323.1 22.5 %copy-start.75 = (bf16[4,1,768]{2,0,1:T(4,128)(2,1)S(1)}, bf16[4,1,768]{2,0,1:T(4,128)(2,1)}, u32[]{:S(2)}) copy-start(bf16[4,1,768]{2,0,1:T(4,128)(2,1)} %param.137) | copy-start | bytes 18436
  323.1 22.5 %copy-start.118 = (s32[3]{0:T(128)S(1)}, s32[3]{0:T(128)}, u32[]{:S(2)}) copy-start(s32[3]{0:T(128)} %constant.1915.clone.1) | copy-start | bytes 40
  327.6 17.9 %copy-start.102 = (bf16[1,768]{1,0:T(2,128)(2,1)}, bf16[1,768]{1,0:T(2,128)(2,1)S(1)}, u32[]{:S(2)}) copy-start(bf16[1,768]{1,0:T(2,128)(2,1)S(1)} %get-tuple-element.1099) | copy-start | bytes 4612
  327.7 31.6 %collective-permute-start.4 = (bf16[513,768]{1,0:T(8,128)(2,1)S(1)}, bf16[513,768]{1,0:T(8,128)(2,1)}, u32[]{:S(2)}, u32[]{:S(2)}) collective-permute-start(bf16[513,768]{1,0:T(8,128)(2,1)S(1)} %pad_maximum_fusion.39), channel_id=1, source_target_pairs={{0,8},{8,16},{16,24},{1,9},{9,17},{17,25},{2,10},{10,18},{18,26},{... | collective-permute-start | bytes 2363912 | tf_op jit(solution)/shard_map/ppermute | solution.py:27
  367.9 18.4 %collective-permute-start.5 = (bf16[513,768]{1,0:T(8,128)(2,1)S(1)}, bf16[513,768]{1,0:T(8,128)(2,1)S(1)}, u32[]{:S(2)}, u32[]{:S(2)}) collective-permute-start(bf16[513,768]{1,0:T(8,128)(2,1)S(1)} %pad_maximum_fusion.40), channel_id=1, source_target_pairs={{0,8},{8,16},{16,24},{1,9},{9,17},{17,25},{2,10},{10,18},{18,26},{... | collective-permute-start | bytes 2363912 | tf_op jit(solution)/shard_map/ppermute | solution.py:27
  414.2 41.3 %copy-start.82 = (bf16[1,768]{1,0:T(2,128)(2,1)}, bf16[1,768]{1,0:T(2,128)(2,1)S(1)}, u32[]{:S(2)}) copy-start(bf16[1,768]{1,0:T(2,128)(2,1)S(1)} %get-tuple-element.1104) | copy-start | bytes 4612
  414.2 41.3 %copy-start.106 = (f32[2,768]{1,0:T(2,128)}, f32[2,768]{1,0:T(2,128)S(1)}, u32[]{:S(2)}) copy-start(f32[2,768]{1,0:T(2,128)S(1)} %get-tuple-element.1124) | copy-start | bytes 18436
  414.2 41.3 %copy-start.76 = (bf16[4,1,768]{2,0,1:T(4,128)(2,1)S(1)}, bf16[4,1,768]{2,0,1:T(4,128)(2,1)}, u32[]{:S(2)}) copy-start(bf16[4,1,768]{2,0,1:T(4,128)(2,1)} %param.137) | copy-start | bytes 18436
  414.2 41.3 %copy-start.5 = (bf16[512,768]{1,0:T(8,128)(2,1)S(1)}, bf16[512,768]{1,0:T(8,128)(2,1)}, u32[]{:S(2)}) copy-start(bf16[512,768]{1,0:T(8,128)(2,1)} %get-tuple-element.1606) | copy-start | bytes 2359300
  414.2 41.3 %copy-start.68 = (bf16[1,768]{1,0:T(2,128)(2,1)S(1)}, bf16[1,768]{1,0:T(2,128)(2,1)}, u32[]{:S(2)}) copy-start(bf16[1,768]{1,0:T(2,128)(2,1)} %get-tuple-element.1599) | copy-start | bytes 4612
  415.5 39.9 %collective-permute-start.6 = (bf16[513,768]{1,0:T(8,128)(2,1)S(1)}, bf16[513,768]{1,0:T(8,128)(2,1)S(1)}, u32[]{:S(2)}, u32[]{:S(2)}) collective-permute-start(bf16[513,768]{1,0:T(8,128)(2,1)S(1)} %pad_maximum_fusion.41), channel_id=1, source_target_pairs={{8,0},{16,8},{24,16},{9,1},{17,9},{25,17},{10,2},{18,10},{26,18},{... | collective-permute-start | bytes 2363912 | tf_op jit(solution)/shard_map/ppermute | solution.py:27
  477.4 19.1 %copy-start.84 = (bf16[1,768]{1,0:T(2,128)(2,1)}, bf16[1,768]{1,0:T(2,128)(2,1)S(1)}, u32[]{:S(2)}) copy-start(bf16[1,768]{1,0:T(2,128)(2,1)S(1)} %get-tuple-element.1106) | copy-start | bytes 4612
  477.5 19.1 %copy-start.108 = (f32[2,768]{1,0:T(2,128)}, f32[2,768]{1,0:T(2,128)S(1)}, u32[]{:S(2)}) copy-start(f32[2,768]{1,0:T(2,128)S(1)} %get-tuple-element.1125) | copy-start | bytes 18436
  477.5 19.0 %copy-start.77 = (bf16[4,1,768]{2,0,1:T(4,128)(2,1)S(1)}, bf16[4,1,768]{2,0,1:T(4,128)(2,1)}, u32[]{:S(2)}) copy-start(bf16[4,1,768]{2,0,1:T(4,128)(2,1)} %param.137) | copy-start | bytes 18436
  477.5 19.0 %copy-start.4 = (bf16[512,768]{1,0:T(8,128)(2,1)S(1)}, bf16[512,768]{1,0:T(8,128)(2,1)}, u32[]{:S(2)}) copy-start(bf16[512,768]{1,0:T(8,128)(2,1)} %get-tuple-element.1605) | copy-start | bytes 2359300
  477.5 19.0 %copy-start.67 = (bf16[1,768]{1,0:T(2,128)(2,1)S(1)}, bf16[1,768]{1,0:T(2,128)(2,1)}, u32[]{:S(2)}) copy-start(bf16[1,768]{1,0:T(2,128)(2,1)} %get-tuple-element.1598) | copy-start | bytes 4612
  478.8 17.6 %collective-permute-start.7 = (bf16[513,768]{1,0:T(8,128)(2,1)S(1)}, bf16[513,768]{1,0:T(8,128)(2,1)S(1)}, u32[]{:S(2)}, u32[]{:S(2)}) collective-permute-start(bf16[513,768]{1,0:T(8,128)(2,1)S(1)} %pad_maximum_fusion.42), channel_id=1, source_target_pairs={{8,0},{16,8},{24,16},{9,1},{17,9},{25,17},{10,2},{18,10},{26,18},{... | collective-permute-start | bytes 2363912 | tf_op jit(solution)/shard_map/ppermute | solution.py:27
  518.6 127.7 %copy-start.86 = (bf16[1,768]{1,0:T(2,128)(2,1)}, bf16[1,768]{1,0:T(2,128)(2,1)S(1)}, u32[]{:S(2)}) copy-start(bf16[1,768]{1,0:T(2,128)(2,1)S(1)} %get-tuple-element.1108) | copy-start | bytes 4612
  518.6 127.7 %copy-start.110 = (f32[2,768]{1,0:T(2,128)}, f32[2,768]{1,0:T(2,128)S(1)}, u32[]{:S(2)}) copy-start(f32[2,768]{1,0:T(2,128)S(1)} %get-tuple-element.1126) | copy-start | bytes 18436
  518.6 127.7 %copy-start.78 = (bf16[4,1,768]{2,0,1:T(4,128)(2,1)S(1)}, bf16[4,1,768]{2,0,1:T(4,128)(2,1)}, u32[]{:S(2)}) copy-start(bf16[4,1,768]{2,0,1:T(4,128)(2,1)} %param.137) | copy-start | bytes 18436
  518.6 127.7 %copy-start.3 = (bf16[512,768]{1,0:T(8,128)(2,1)S(1)}, bf16[512,768]{1,0:T(8,128)(2,1)}, u32[]{:S(2)}) copy-start(bf16[512,768]{1,0:T(8,128)(2,1)} %get-tuple-element.1604) | copy-start | bytes 2359300
  518.6 127.7 %copy-start.66 = (bf16[1,768]{1,0:T(2,128)(2,1)S(1)}, bf16[1,768]{1,0:T(2,128)(2,1)}, u32[]{:S(2)}) copy-start(bf16[1,768]{1,0:T(2,128)(2,1)} %get-tuple-element.1597) | copy-start | bytes 4612
  519.9 126.3 %collective-permute-start.8 = (bf16[513,768]{1,0:T(8,128)(2,1)S(1)}, bf16[513,768]{1,0:T(8,128)(2,1)S(1)}, u32[]{:S(2)}, u32[]{:S(2)}) collective-permute-start(bf16[513,768]{1,0:T(8,128)(2,1)S(1)} %pad_maximum_fusion.43), channel_id=1, source_target_pairs={{8,0},{16,8},{24,16},{9,1},{17,9},{25,17},{10,2},{18,10},{26,18},{... | collective-permute-start | bytes 2363912 | tf_op jit(solution)/shard_map/ppermute | solution.py:27
  750.8 17.3 %copy-start.88 = (bf16[1,768]{1,0:T(2,128)(2,1)}, bf16[1,768]{1,0:T(2,128)(2,1)S(1)}, u32[]{:S(2)}) copy-start(bf16[1,768]{1,0:T(2,128)(2,1)S(1)} %get-tuple-element.1110) | copy-start | bytes 4612
  750.8 17.3 %copy-start.112 = (f32[2,768]{1,0:T(2,128)}, f32[2,768]{1,0:T(2,128)S(1)}, u32[]{:S(2)}) copy-start(f32[2,768]{1,0:T(2,128)S(1)} %get-tuple-element.1127) | copy-start | bytes 18436
  750.8 17.2 %copy-start.79 = (bf16[4,1,768]{2,0,1:T(4,128)(2,1)S(1)}, bf16[4,1,768]{2,0,1:T(4,128)(2,1)}, u32[]{:S(2)}) copy-start(bf16[4,1,768]{2,0,1:T(4,128)(2,1)} %param.137) | copy-start | bytes 18436
  750.8 17.2 %copy-start.2 = (bf16[512,768]{1,0:T(8,128)(2,1)S(1)}, bf16[512,768]{1,0:T(8,128)(2,1)}, u32[]{:S(2)}) copy-start(bf16[512,768]{1,0:T(8,128)(2,1)} %get-tuple-element.1603) | copy-start | bytes 2359300
  750.8 17.2 %copy-start.65 = (bf16[1,768]{1,0:T(2,128)(2,1)S(1)}, bf16[1,768]{1,0:T(2,128)(2,1)}, u32[]{:S(2)}) copy-start(bf16[1,768]{1,0:T(2,128)(2,1)} %get-tuple-element.1596) | copy-start | bytes 4612
  752.1 15.8 %collective-permute-start.9 = (bf16[513,768]{1,0:T(8,128)(2,1)S(1)}, bf16[513,768]{1,0:T(8,128)(2,1)S(1)}, u32[]{:S(2)}, u32[]{:S(2)}) collective-permute-start(bf16[513,768]{1,0:T(8,128)(2,1)S(1)} %pad_maximum_fusion.44), channel_id=1, source_target_pairs={{8,0},{16,8},{24,16},{9,1},{17,9},{25,17},{10,2},{18,10},{26,18},{... | collective-permute-start | bytes 2363912 | tf_op jit(solution)/shard_map/ppermute | solution.py:27
  873.9 14.9 %collective-permute-start.10 = (bf16[513,768]{1,0:T(8,128)(2,1)S(1)}, bf16[513,768]{1,0:T(8,128)(2,1)S(1)}, u32[]{:S(2)}, u32[]{:S(2)}) collective-permute-start(bf16[513,768]{1,0:T(8,128)(2,1)S(1)} %pad_maximum_fusion.45), channel_id=1, source_target_pairs={{8,0},{16,8},{24,16},{9,1},{17,9},{25,17},{10,2},{18,10},{26,18},{... | collective-permute-start | bytes 2363912 | tf_op jit(solution)/shard_map/ppermute | solution.py:27
  994.8 14.0 %collective-permute-start.11 = (bf16[513,768]{1,0:T(8,128)(2,1)S(1)}, bf16[513,768]{1,0:T(8,128)(2,1)S(1)}, u32[]{:S(2)}, u32[]{:S(2)}) collective-permute-start(bf16[513,768]{1,0:T(8,128)(2,1)S(1)} %pad_maximum_fusion.46), channel_id=1, source_target_pairs={{8,0},{16,8},{24,16},{9,1},{17,9},{25,17},{10,2},{18,10},{26,18},{... | collective-permute-start | bytes 2363912 | tf_op jit(solution)/shard_map/ppermute | solution.py:27
  1165.2 29.4 %all-to-all-start = ((bf16[4,2,384]{2,1,0:T(2,128)(2,1)}), bf16[4,2,384]{2,1,0:T(2,128)(2,1)S(1)}, u32[]{:S(2)}, u32[]{:S(2)}) async-start(bf16[4,2,384]{2,1,0:T(2,128)(2,1)} %reshape.5883), calls=%async_computation | async-start | bytes 12288 | tf_op jit(solution)/shard_map/all_to_all | solution.py:405
  1194.6 17.2 %all-to-all-start.2 = ((bf16[4,2,384]{2,1,0:T(2,128)(2,1)}), bf16[4,2,384]{2,1,0:T(2,128)(2,1)S(1)}, u32[]{:S(2)}, u32[]{:S(2)}) async-start(bf16[4,2,384]{2,1,0:T(2,128)(2,1)} %reshape.5885), calls=%async_computation.2 | async-start | bytes 12288 | tf_op jit(solution)/shard_map/all_to_all | solution.py:407
  1211.8 69.7 %all-to-all-start.1 = ((bf16[4,512,768]{2,1,0:T(8,128)(2,1)}), bf16[4,512,768]{2,1,0:T(8,128)(2,1)S(1)}, u32[]{:S(2)}, u32[]{:S(2)}) async-start(bf16[4,512,768]{2,1,0:T(8,128)(2,1)} %fusion.1791), calls=%async_computation.1 | async-start | bytes 6291456 | tf_op jit(solution)/shard_map/all_to_all | solution.py:406
  1215.5 61.5 %reduce-scatter.7.cloned.1.call-start = ((), (), s32[]{:S(2)}) async-start(), calls=%async_computation.8 | async-start | bytes 245760
  1216.5 84.3 %all-reduce.9.cloned.1.call-start = ((), (), s32[]{:S(2)}) async-start(), calls=%async_computation.6 | async-start | bytes 4718592 | tf_op jit(solution)/shard_map/psum | solution.py:418
  (65 other events, 544.4 us)
Sparse Core Ops, SparseCore 0:
  9.9 99.0 all-gather.2
  1157.3 92.3 reduce-scatter.4
  1253.0 23.9 reduce-scatter.6
  1279.2 21.5 all-reduce.8
where the time goes:
time: 1320 us; the launch traced here: 1310 us
  waiting for transfers between devices  489 us (37%)
  matrix products  301 us (23%)
  loops' own time  187 us (14%)
  other arithmetic  143 us (11%)
  local copies, waits for them, and re-layouts  126 us (10%)
  starting transfers between devices  47.8 us (4%)
  between operations  16.2 us (1%)
    ppermute x12, waiting for transfers between devices, shifted(): lax.ppermute(value, axis, [(source, source + steps) for source in range(i...  302 us
    another operation x7, loops' own time, body(): lax.switch(branch, backward_table, saved[:rows], saved[rows:], lengths[sl...  145 us
    all_gather x1, waiting for transfers between devices, body(): weight_cols = lax.all_gather(weights[0], 'pair', axis=1, tiled=True)  97.2 us
    dot_general x28, matrix products, matmul(): return jnp.dot(left, right, preferred_element_type=jnp.float32)  71.6 us
    sub x8, matrix products, encoder_forward(): soft_probs = jax.nn.softmax(scores, axis=-1)  59.4 us
    convert_element_type x1, other arithmetic, body(): grads_weight.astype(jnp.bfloat16)  44.5 us
    another operation x7, loops' own time, body(): lax.switch(branch, forward_table, enc_x, dec_x, lengths[slot], weight_col...  42 us
    dot_general x16, matrix products, outer_sum(): lax.dot_general(left, right, (((0,), (0,)), ((), ())), preferred_element_...  38.2 us
  transfers between devices with their start and end apart: 19, of which 17 were waited for; matrix products, arithmetic and copies ran while one was open for 4% of the time, Pallas kernels for 0%

commit v1 on v0

v1 whole, which is shorter than its diff:
```python
import jax
import jax.numpy as jnp
from jax import lax
from jax.experimental import pallas as pl
from jax.experimental.pallas import tpu as pltpu
from jax.sharding import PartitionSpec as P

D = 768
HALF = 384
K = 4
R = HALF // K
MESH = pl.DeviceIdType.MESH


def loop(n, go):
    lax.fori_loop(0, n, go, 0)


def place():
    s, p, d = lax.axis_index("section"), lax.axis_index("pair"), lax.axis_index("dp")
    c = lax.rem(d, 2)
    xn = p + 1 - 2 * lax.rem(p, 2)
    yn = p + 2 - 4 * (p // 2)
    return s, p, d, c, xn, yn, 3 - p, d + 1 - 2 * c


def enter(s, p, d, xn, yn, dn):
    bar = pltpu.get_barrier_semaphore()

    def tell(target):
        pl.semaphore_signal(bar, inc=1, device_id=target, device_id_type=MESH)

    tell((s, xn, d))
    tell((s, yn, d))
    tell((s, p, dn))
    pl.when(s < 3)(lambda: tell((s + 1, p, d)))
    pl.when(s > 0)(lambda: tell((s - 1, p, d)))
    pl.semaphore_wait(bar, 5 - (3 - s) // 3 - s // 3)


X, Y, UP, DOWN = 0, 1, 2, 3


def gather_kernel(w_ref, out_ref, buf, ssem, rsem, csend, crecv, lsem):
    s, p, d, c, xn, yn, dg, dn = place()

    def part(b, k):
        return buf.at[b, pl.ds(pl.multiple_of(c * HALF + k * R, R), R), :]

    targets = {X: (s, xn, d), Y: (s, yn, d), UP: (s + 1, p, d), DOWN: (s - 1, p, d)}

    def copy(link, b, k):
        return pltpu.make_async_remote_copy(
            src_ref=part(b, k), dst_ref=part(b, k), send_sem=ssem.at[link, b, k], recv_sem=rsem.at[b, k],
            device_id=targets[link], device_id_type=MESH)

    def sibling(b, k):
        return pltpu.make_async_remote_copy(
            src_ref=part(b, k), dst_ref=part(b, k), send_sem=csend.at[b, k], recv_sem=crecv.at[b],
            device_id=(s, p, dn), device_id_type=MESH)

    def got(b, k):
        copy(X, b, k).wait_recv()
        sibling(b, k).start()

    def local(j):
        index = jnp.where(s == 0, p + 2 * j, 4 * (1 + j) + p)
        return pltpu.make_async_copy(w_ref.at[:, pl.ds(j * D, D)], buf.at[index], lsem.at[j])

    is0, is1 = s == 0, s == 1
    has = (is0 & (p < 2)) | is1

    @pl.when(has)
    def _():
        local(0).start()
        local(1).start()
        local(0).wait()
        local(1).wait()

    enter(s, p, d, xn, yn, dn)

    @pl.when(is1)
    def _():
        def go(t, _):
            copy(DOWN, 4 * (1 + t // K) + p, lax.rem(t, K)).start()
            return 0
        loop(2 * K, go)
        copy(UP, 4 + p, 0).start()
        copy(X, 4 + p, 0).start()
        copy(Y, 4 + p, 0).start()

    xb = lax.rem(p, 2)

    @pl.when(is0)
    def _():
        def go(t, _):
            h, k = t // K, lax.rem(t, K)
            b = xb + 2 - 2 * h
            @pl.when(p < 2)
            def _():
                @pl.when(t > 1)
                def _():
                    h2, k2 = (t - 2) // K, lax.rem(t - 2, K)
                    copy(Y, xb + 2 - 2 * h2, k2).wait_send()
                    copy(X, xb + 2 - 2 * h2, k2).wait_send()
                copy(Y, b, k).start()
                copy(X, b, k).start()
                pl.when(t < K)(lambda: copy(UP, p, k).start())

            @pl.when(p >= 2)
            def _():
                got(b, k)
                pl.when(t < K)(lambda: copy(UP, p, k).start())
                copy(X, b, k).start()

            @pl.when(t > 1)
            def _():
                h2, k2 = (t - 2) // K, lax.rem(t - 2, K)
                got(3 - xb - 2 * h2, k2)
            return 0
        loop(2 * K, go)
        got(1 - xb, K - 2)
        got(1 - xb, K - 1)

        def w1(t, _):
            b, k = 4 * (1 + t // K) + p, lax.rem(t, K)
            got(b, k)
            copy(X, b, k).start()
            copy(Y, b, k).start()
            return 0
        loop(2 * K, w1)

        def rest(t, _):
            b0, k = 4 * (1 + t // K), lax.rem(t, K)
            got(b0 + xn, k)
            got(b0 + yn, k)
            got(b0 + dg, k)
            return 0
        loop(2 * K, rest)

    @pl.when(s > 0)
    def _():
        def go(t, _):
            @pl.when(t < 3 * K)
            def _():
                b, k = 4 * (t // K) + p, lax.rem(t, K)
                mine = is1 & (t >= K)
                pl.when(jnp.logical_not(mine))(lambda: got(b, k))

                @pl.when(jnp.logical_not(is1 & (t == K)))
                def _():
                    pl.when(s < 3)(lambda: copy(UP, b, k).start())
                    copy(X, b, k).start()
                    copy(Y, b, k).start()

            @pl.when((t > 1) & (t < 3 * K + 2))
            def _():
                b0, k = 4 * ((t - 2) // K), lax.rem(t - 2, K)
                got(b0 + xn, k)
                pl.when(lax.rem(k, 2) == 0)(lambda: copy(Y, b0 + xn, k).start())
                got(b0 + yn, k)
                pl.when(lax.rem(k, 2) == 1)(lambda: copy(X, b0 + yn, k).start())

            @pl.when(t > 3)
            def _():
                b0, k = 4 * ((t - 4) // K), lax.rem(t - 4, K)
                got(b0 + dg, k)
                pl.when(is1 & (b0 > 0))(lambda: copy(DOWN, b0 + dg, k).start())
            return 0

        loop(3 * K + 4, go)

    def sent(b, cond, link):
        def go(k, _):
            copy(link, b, k).wait_send()
            return 0
        pl.when(cond)(lambda: loop(K, go))

    @pl.when(is0)
    def _():
        @pl.when(p < 2)
        def _():
            for k in (K - 2, K - 1):
                copy(X, xb, k).wait_send()
                copy(Y, xb, k).wait_send()
        sent(xb, p >= 2, X)
        sent(xb + 2, p >= 2, X)
        sent(p, p >= 0, UP)

    @pl.when(s > 0)
    def _():
        sent(p, s < 3, UP)
        sent(p, s < 4, X)
        sent(p, s < 4, Y)

    def relayed(b0):
        def go(k, _):
            copy(Y, b0 + xn, 2 * k).wait_send()
            copy(X, b0 + yn, 2 * k + 1).wait_send()
            return 0
        loop(K // 2, go)

    pl.when(s > 0)(lambda: relayed(0))
    for j in range(2):
        b = 4 * (1 + j) + p
        sent(b, (s == 1) | (s == 2), UP)
        sent(b, s < 4, X)
        sent(b, s < 4, Y)
        sent(b, is1, DOWN)
        sent(4 * (1 + j) + dg, is1, DOWN)
        pl.when(s > 0)(lambda j=j: relayed(4 * (1 + j)))

    def whole(b, _):
        mine = (is0 & (p < 2) & (b < 4) & (lax.rem(b, 2) == p)) | (is1 & (b >= 4) & (lax.rem(b, 4) == p))

        @pl.when(jnp.logical_not(mine))
        def _():
            def go(k, _):
                sibling(b, k).wait_send()
                return 0
            loop(K, go)
            other = buf.at[b, pl.ds(pl.multiple_of((1 - c) * HALF, HALF), HALF), :]
            pltpu.make_async_remote_copy(
                src_ref=other, dst_ref=other, send_sem=csend.at[b, 0], recv_sem=crecv.at[b],
                device_id=(s, p, dn), device_id_type=MESH).wait_recv()
        return 0

    loop(12, whole)
    out = pltpu.make_async_copy(buf, out_ref, lsem.at[0])
    out.start()
    out.wait()


def gather(w):
    return pl.pallas_call(
        gather_kernel,
        out_shape=jax.ShapeDtypeStruct((12, D, D), jnp.bfloat16),
        in_specs=[pl.BlockSpec(memory_space=pl.ANY)],
        out_specs=pl.BlockSpec(memory_space=pl.ANY),
        scratch_shapes=[
            pltpu.VMEM((12, D, D), jnp.bfloat16),
            pltpu.SemaphoreType.DMA((4, 12, K)),
            pltpu.SemaphoreType.DMA((12, K)),
            pltpu.SemaphoreType.DMA((12, K)),
            pltpu.SemaphoreType.DMA((12,)),
            pltpu.SemaphoreType.DMA((2,)),
        ],
        compiler_params=pltpu.CompilerParams(collective_id=0, has_side_effects=True, vmem_limit_bytes=60<<20),
        name="gather",
    )(w)


def reduce_kernel(g_ref, fin_out, cb, sr, rr, ox, oy, zu, zd, fin, ssib, rsib, sxy, sz, sfy, sfib, r_rr, r_ox, r_oy, r_zu, r_zd, r_fy, r_fib, lsem):
    s, p, d, c, xn, yn, dg, dn = place()
    is0, is1 = s == 0, s == 1
    XN, YN, UPN, DNN, SIB = (s, xn, d), (s, yn, d), (s + 1, p, d), (s - 1, p, d), (s, p, dn)

    cp = pltpu.make_async_copy(g_ref, cb, lsem.at[0])
    cp.start()
    cp.wait()
    enter(s, p, d, xn, yn, dn)

    def remote(src, dst, ss, rs, to):
        return pltpu.make_async_remote_copy(src_ref=src, dst_ref=dst, send_sem=ss, recv_sem=rs, device_id=to, device_id_type=MESH)

    def mine(b, k):
        return cb.at[b, pl.ds(pl.multiple_of(c * HALF + k * R, R), R), :]

    def other(b, k):
        return cb.at[b, pl.ds(pl.multiple_of((1 - c) * HALF + k * R, R), R), :]

    def srow(b, k):
        return sr.at[b, pl.ds(pl.multiple_of(k * R, R), R), :]

    def sib(b, k):
        return remote(other(b, k), srow(b, k), ssib.at[b, k], rsib.at[b, k], SIB)

    def even(k):
        return lax.rem(k, 2) == 0

    def diag(st, k, y):
        return remote(mine(4 * st + dg, k), rr.at[st, k], sxy.at[0, st, k], r_rr.at[st, k], YN if y else XN)

    def direct(st, k, y):
        return remote(mine(4 * st + (yn if y else xn), k), (oy if y else ox).at[st, k], sxy.at[1, st, k], (r_oy if y else r_ox).at[st, k], YN if y else XN)

    def relay(st, k, y):
        return remote(mine(4 * st + (yn if y else xn), k), (oy if y else ox).at[st, k], sxy.at[2, st, k], (r_oy if y else r_ox).at[st, k], YN if y else XN)

    def both(k, f):
        pl.when(even(k))(lambda: f(0))
        pl.when(jnp.logical_not(even(k)))(lambda: f(1))

    def first(st, k):
        for q in (dg, xn, yn, p):
            sib(4 * st + q, k).wait_recv()
            m = mine(4 * st + q, k)
            m[...] = (f32(m[...]) + f32(srow(4 * st + q, k)[...])).astype(jnp.bfloat16)

        def f(odd):
            diag(st, k, not odd).start()
            direct(st, k, not odd).start()
        both(k, f)

    def second(st, k):
        diag(st, k, True).wait_recv()

        def f(odd):
            m = mine(4 * st + (yn if odd else xn), k)
            m[...] = (f32(m[...]) + f32(rr[st, k])).astype(jnp.bfloat16)
            relay(st, k, odd).start()
        both(k, f)

    def up(st, k):
        return remote(mine(4 * st + p, k), zd.at[st, k], sz.at[st, k], r_zd.at[st, k], UPN)

    def down(st, k):
        return remote(mine(4 * st + p, k), zu.at[st, k], sz.at[st, k], r_zu.at[st, k], DNN)

    def third(st, k):
        direct(st, k, True).wait_recv()
        direct(st, k, False).wait_recv()
        m = mine(4 * st + p, k)
        return m, f32(m[...]) + f32(ox[st, k]) + f32(oy[st, k])

    def finrow(j, k):
        return fin.at[j, pl.ds(pl.multiple_of(c * HALF + k * R, R), R), :]

    def fsib(j, k):
        return remote(finrow(j, k), finrow(j, k), sfib.at[j, k], r_fib.at[j, k], SIB)

    def finy(k):
        return remote(finrow(0, k), finrow(1, k), sfy.at[k], r_fy.at[k], YN)

    def last1(st, k):
        m, total = third(st, k)

        @pl.when((s == 3) | is0)
        def _():
            m[...] = total.astype(jnp.bfloat16)
            pl.when(s == 3)(lambda: down(st, k).start())
            pl.when(is0)(lambda: up(st, k).start())

        @pl.when(s == 2)
        def _():
            down(st, k).wait_recv()
            m[...] = (total + f32(zu[st, k])).astype(jnp.bfloat16)
            down(st, k).start()

        @pl.when(is1)
        def _():
            down(st, k).wait_recv()
            up(st, k).wait_recv()
            finrow(st - 1, k)[...] = (total + f32(zu[st, k]) + f32(zd[st, k])).astype(jnp.bfloat16)
            fsib(st - 1, k).start()

    def last0(k):
        m, total = third(0, k)

        @pl.when(s == 3)
        def _():
            m[...] = total.astype(jnp.bfloat16)
            down(0, k).start()

        @pl.when((s == 1) | (s == 2))
        def _():
            down(0, k).wait_recv()
            m[...] = (total + f32(zu[0, k])).astype(jnp.bfloat16)
            down(0, k).start()

        @pl.when(is0)
        def _():
            down(0, k).wait_recv()
            finrow(0, k)[...] = (total + f32(zu[0, k])).astype(jnp.bfloat16)
            pl.when(p < 2)(lambda: fsib(0, k).start())
            pl.when(p >= 2)(lambda: finy(k).start())

    def send_sib(t, _):
        st, k = lax.rem(t // K + 1, 3), lax.rem(t, K)
        for q in (dg, xn, yn, p):
            sib(4 * st + q, k).start()
        return 0

    loop(3 * K, send_sib)

    lag1 = 6 - s - 3 * ((3 - s) // 3)
    lag0 = 6 - s

    def step(t, _):
        pl.when(t < 3 * K)(lambda: first(lax.rem(t // K + 1, 3), lax.rem(t, K)))
        pl.when((t >= 1) & (t < 3 * K + 1))(lambda: second(lax.rem((t - 1) // K + 1, 3), lax.rem(t - 1, K)))
        t1 = t - lag1
        pl.when((t1 >= 0) & (t1 < 2 * K))(lambda: last1(1 + t1 // K, lax.rem(t1, K)))
        t0 = t - lag0
        pl.when((t0 >= 2 * K) & (t0 < 3 * K))(lambda: last0(t0 - 2 * K))
        return 0

    loop(3 * K + 7, step)

    @pl.when(is0 & (p < 2))
    def _():
        def go(k, _):
            finy(k).wait_recv()
            fsib(1, k).start()
            return 0
        loop(K, go)

    @pl.when(is1 | (is0 & (p < 2)))
    def _():
        def go(t, _):
            j, k = t // K, lax.rem(t, K)
            fsib(j, k).wait()
            return 0
        loop(2 * K, go)

    @pl.when(is0 & (p >= 2))
    def _():
        def go(k, _):
            finy(k).wait_send()
            return 0
        loop(K, go)

    def drain(t, _):
        st, k = t // K, lax.rem(t, K)
        for q in range(4):
            sib(4 * st + q, k).wait_send()
        diag(st, k, True).wait_send()
        direct(st, k, True).wait_send()
        relay(st, k, True).wait_send()
        pl.when((st > 0) & (s != 1))(lambda: down(st, k).wait_send())
        pl.when((st == 0) & (s > 0))(lambda: down(st, k).wait_send())
        return 0

    loop(3 * K, drain)
    cp = pltpu.make_async_copy(fin, fin_out, lsem.at[0])
    cp.start()
    cp.wait()


def reduce(g):
    bf = jnp.bfloat16
    dma = pltpu.SemaphoreType.DMA
    return pl.pallas_call(
        reduce_kernel,
        out_shape=jax.ShapeDtypeStruct((2, D, D), bf),
        in_specs=[pl.BlockSpec(memory_space=pl.ANY)],
        out_specs=pl.BlockSpec(memory_space=pl.ANY),
        scratch_shapes=[
            pltpu.VMEM((12, D, D), bf), pltpu.VMEM((12, HALF, D), bf),
            pltpu.VMEM((3, K, R, D), bf), pltpu.VMEM((3, K, R, D), bf), pltpu.VMEM((3, K, R, D), bf),
            pltpu.VMEM((3, K, R, D), bf), pltpu.VMEM((3, K, R, D), bf), pltpu.VMEM((2, D, D), bf),
            dma((12, K)), dma((12, K)), dma((3, 3, K)), dma((3, K)), dma((K,)), dma((2, K)),
            dma((3, K)), dma((3, K)), dma((3, K)), dma((3, K)), dma((3, K)), dma((K,)), dma((2, K)), dma((1,)),
        ],
        compiler_params=pltpu.CompilerParams(collective_id=1, has_side_effects=True, vmem_limit_bytes=60 << 20),
        name="reduce",
    )(g)


HEADS = 12
HEAD = 64
FF = 3072
L = 512
EPSILON = 1e-06
NEGATIVE = -1e30
ALL = ("section", "pair", "dp")


def f32(v):
    return v.astype(jnp.float32)


def bf16(v):
    return v.astype(jnp.bfloat16)


def norm(v, g):
    return v * lax.rsqrt(jnp.mean(v * v, axis=-1, keepdims=True) + EPSILON) * g


def norm_back(v, g, c):
    r = lax.rsqrt(jnp.mean(v * v, axis=-1, keepdims=True) + EPSILON)
    gc = g * c
    return r * gc - v * (r * r * r) * jnp.mean(v * gc, axis=-1, keepdims=True), jnp.sum(r * v * c, axis=0)


def gelu_both(u):
    a = 0.7978845608028654
    t = jnp.tanh(a * (u + 0.044715 * u * u * u))
    return 0.5 * u * (1.0 + t), 0.5 * (1.0 + t) + 0.5 * u * (1.0 - t * t) * a * (1.0 + 0.134145 * u * u)


def nn(a, b):
    return jnp.dot(a, b, preferred_element_type=jnp.float32)


def nt(a, b):
    return lax.dot_general(a, b, (((1,), (1,)), ((), ())), preferred_element_type=jnp.float32)


def tn(a, b):
    return lax.dot_general(a, b, (((0,), (0,)), ((), ())), preferred_element_type=jnp.float32)


def on(v, s, p):
    here = (lax.axis_index("section") == s) & (lax.axis_index("pair") == p)
    return lax.psum(jnp.where(here, v, jnp.zeros_like(v)), ("section", "pair"))


def spread(rows):
    head = lax.broadcasted_iota(jnp.int32, (16, D), 1) // HEAD == lax.broadcasted_iota(jnp.int32, (16, D), 0)
    return jnp.where(head[None], rows[:, None, :], jnp.zeros((), rows.dtype))


def body(enc_in, dec_in, lengths, weights, gains, dec_cot):
    s, p, d = lax.axis_index("section"), lax.axis_index("pair"), lax.axis_index("dp")
    pairs, dps = lax.axis_size("pair"), lax.axis_size("dp")
    me = (s * pairs + p) * dps + d
    w = weights[0]
    g = lax.all_gather(gains[0], "section")
    blocks = gather(w)
    x = f32(lax.dynamic_index_in_dim(enc_in, s, 0, False))
    dec_x = f32(lax.dynamic_index_in_dim(dec_in, s, 0, False))
    cot = f32(lax.dynamic_index_in_dim(dec_cot, s, 0, False))
    length = lax.dynamic_index_in_dim(lengths, s, 0, False)[0]
    live = lax.broadcasted_iota(jnp.int32, (1, L), 1) < length
    scale = HEAD ** -0.5

    normed = bf16(norm(x, g[0, 0]))

    def heads(v):
        return v.reshape(L, HEADS, HEAD)

    q, v, k, wo = (blocks[i] for i in range(4))
    q, k, v = bf16(nn(normed, q)), bf16(nn(normed, k)), bf16(nn(normed, v))
    scores = jnp.einsum("qhd,khd->hqk", heads(q), heads(k), preferred_element_type=jnp.float32) * scale
    probs = jax.nn.softmax(jnp.where(live[None], scores, NEGATIVE), axis=-1)
    low = bf16(probs)
    att = bf16(jnp.einsum("hqk,khd->qhd", low, heads(v), preferred_element_type=jnp.float32)).reshape(L, D)
    enc0 = bf16(x + nt(att, wo))
    e0 = f32(enc0)
    fnorm = bf16(norm(e0, g[1, 0]))
    up = [blocks[4], blocks[8], blocks[5], blocks[9]]
    dn = [blocks[6], blocks[10], blocks[7], blocks[11]]
    hid, act = [], []
    mid = e0
    for i in range(4):
        hid.append(nn(fnorm, up[i]))
        act.append(bf16(gelu_both(hid[i])[0]))
        mid = mid + nt(act[i], dn[i])
    enc = bf16(norm(mid, g[1, 1]))

    wa, wb = w[:, :D], w[:, D:]
    dec_rows = lax.all_gather(dec_x, ALL, tiled=True)
    cot_rows = lax.all_gather(cot, ALL, tiled=True)
    n = dec_rows.shape[0]
    dnorm = bf16(norm(dec_rows, g[2, 0]))
    self_v = bf16(nn(dnorm, wa))
    self_v = on(self_v, 2, 0)
    dmid = on(dec_rows + nt(self_v, wb), 2, 0)
    cnorm = bf16(norm(dmid, g[2, 1]))
    cq = on(bf16(nn(cnorm, wa)), 2, 1)
    u = on(bf16(nt(spread(cq).reshape(n * 16, D), wb)), 2, 1).reshape(n, 16, D)
    u = lax.dynamic_index_in_dim(u, me, 0, False)
    cs = jnp.where(live, nt(u, enc) * scale, NEGATIVE)
    cp = jax.nn.softmax(cs, axis=-1)
    clow = bf16(cp)
    z = bf16(nn(clow, enc))
    z_all = lax.all_gather(z, ALL)
    head = spread(jnp.ones((1, D), jnp.float32))[0]
    catt = on(bf16(jnp.sum(nn(z_all.reshape(n * 16, D), wa).reshape(n, 16, D) * head, axis=1)), 2, 2)
    decoded = bf16(on(dmid + nt(catt, wb), 2, 2))
    dec32 = f32(decoded)
    tnorm = bf16(norm(dec32, g[3, 0]))
    thid = nn(tnorm, w)
    thid = lax.ppermute(thid, "pair", [(0, 2), (1, 3)])
    ta, td = gelu_both(thid)
    tact = bf16(ta)
    downs = (s == 3) & (p >= 2)
    tmid = dec32 + lax.psum(jnp.where(downs, nt(tact, w), 0.0), ("section", "pair"))
    dec_out = bf16(norm(tmid, g[3, 1]))
    g_tmid, gg31 = norm_back(tmid, g[3, 1], cot_rows)
    g_tb = bf16(g_tmid)
    g_thid = bf16(td * nn(g_tb, w))
    g_thid_up = lax.ppermute(g_thid, "pair", [(2, 0), (3, 1)])
    g_tn = lax.psum(jnp.where((s == 3) & (p < 2), nt(g_thid_up, w), 0.0), ("section", "pair"))
    gp, gg30 = norm_back(dec32, g[3, 0], g_tn)
    g_dec = bf16(g_tmid + gp)
    dw3 = jnp.where(p < 2, tn(tnorm, g_thid_up), tn(g_tb, tact))
    g_catt = on(bf16(nn(g_dec, wb)), 2, 2)
    vv = on(bf16(nt(spread(g_catt).reshape(n * 16, D), wa)), 2, 2).reshape(n, 16, D)
    vv = lax.dynamic_index_in_dim(vv, me, 0, False)
    g_cp = nt(vv, enc)
    g_cs = bf16(cp * (g_cp - jnp.sum(g_cp * cp, axis=-1, keepdims=True)))
    y = bf16(nn(g_cs, enc) * scale)
    g_enc = bf16(tn(g_cs, bf16(f32(u) * scale)) + tn(clow, vv))
    y_all = lax.all_gather(y, ALL)
    g_cq = on(bf16(jnp.sum(nn(y_all.reshape(n * 16, D), wb).reshape(n, 16, D) * head, axis=1)), 2, 1)
    g_cn = on(nt(g_cq, wa), 2, 1)
    gp, gg21 = norm_back(dmid, g[2, 1], g_cn)
    g_dmid = f32(g_dec) + gp
    g_sb = bf16(g_dmid)
    g_sv = on(bf16(nn(g_sb, wb)), 2, 0)
    g_dn = on(nt(g_sv, wa), 2, 0)
    gp, gg20 = norm_back(dec_rows, g[2, 0], g_dn)
    dec_grad = bf16(g_dmid + gp)
    yz = lax.dynamic_index_in_dim(jnp.stack([y_all, z_all]), jnp.clip(p - 1, 0, 1), 0, False).reshape(n * 16, D)
    dw_a = jnp.where(p == 0, tn(dnorm, g_sv), jnp.where(p == 1, tn(cnorm, g_cq), tn(yz, spread(g_catt).reshape(n * 16, D))))
    dw_b = jnp.where(p == 0, tn(g_sb, self_v), jnp.where(p == 1, tn(yz, spread(cq).reshape(n * 16, D)), tn(g_dec, catt)))
    dw2 = jnp.where(p == 3, 0.0, jnp.concatenate([dw_a, dw_b], axis=1))

    g_mid, gg11 = norm_back(mid, g[1, 1], f32(g_enc))
    g_fb = bf16(g_mid)
    g_fn = jnp.zeros((L, D), jnp.float32)
    d_up, d_dn = [], []
    for i in range(4):
        gh = bf16(gelu_both(hid[i])[1] * nn(g_fb, dn[i]))
        d_up.append(bf16(tn(fnorm, gh)))
        d_dn.append(bf16(tn(g_fb, act[i])))
        g_fn = g_fn + nt(gh, up[i])
    gp, gg10 = norm_back(e0, g[1, 0], g_fn)
    g_e0 = bf16(g_mid + gp)
    g_att = bf16(nn(g_e0, wo))
    d_wo = bf16(tn(g_e0, att))
    g_v = bf16(jnp.einsum("hqk,qhd->khd", low, heads(g_att), preferred_element_type=jnp.float32)).reshape(L, D)
    g_p = jnp.einsum("qhd,khd->hqk", heads(g_att), heads(v), preferred_element_type=jnp.float32)
    g_s = bf16(probs * (g_p - jnp.sum(g_p * probs, axis=-1, keepdims=True)))
    g_q = bf16(jnp.einsum("hqk,khd->qhd", g_s, heads(k), preferred_element_type=jnp.float32) * scale).reshape(L, D)
    g_k = bf16(jnp.einsum("hqk,qhd->khd", g_s, heads(q), preferred_element_type=jnp.float32) * scale).reshape(L, D)
    g_n = nt(g_q, blocks[0]) + nt(g_k, blocks[2]) + nt(g_v, blocks[1])
    gp, gg00 = norm_back(x, g[0, 0], g_n)
    enc_grad = bf16(f32(g_e0) + gp)
    grads = jnp.stack([bf16(tn(normed, g_q)), bf16(tn(normed, g_v)), bf16(tn(normed, g_k)), d_wo,
                       d_up[0], d_up[2], d_dn[0], d_dn[2], d_up[1], d_up[3], d_dn[1], d_dn[3]])
    fin = reduce(grads)
    if dps > 2:
        groups = [[i for i in range(dps) if i % 2 == c] for c in range(2)]
        fin = bf16(lax.psum(fin, "dp", axis_index_groups=groups))
    full = f32(jnp.concatenate([fin[0], fin[1]], axis=1))
    dw = jnp.where(s == 0, jnp.where(p < 2, full, 0.0), jnp.where(s == 1, full, jnp.where(s == 2, dw2, dw3)))
    zero = jnp.zeros((D,), jnp.float32)
    part = lax.psum(jnp.stack([gg00, zero, gg10, gg11]).reshape(2, 2, D), ALL)
    gg = jnp.concatenate([part, jnp.stack([gg20, gg21, gg30, gg31]).reshape(2, 2, D)])
    gg = lax.dynamic_index_in_dim(gg, s, 0, False)
    width = D // pairs
    gg = lax.dynamic_slice_in_dim(gg, p * width, width, 1)
    own = lambda a: lax.dynamic_index_in_dim(a, me, 0, False)[None, None]
    return own(dec_out), enc_grad[None], own(dec_grad), dw[None], gg[None]


def solution(mesh):
    rows, both = P(None, ("pair", "dp"), None), P("section", ("pair", "dp"), None)
    return jax.shard_map(
        body, mesh=mesh,
        in_specs=(rows, rows, P(None, ("pair", "dp")), P("section", None, "pair"), P("section", None, None), rows),
        out_specs=(both, both, both, P("section", None, "pair"), P("section", None, "pair")),
        check_vma=False)
```

time: 1320 us -> 1630 us (1.23)
  blocking collectives: 2.47 us -> 739 us
  loops' own time: 187 us -> 0 us
  Pallas kernels: 0 us -> 179 us
  matrix products: 301 us -> 171 us
  local copies, waits for them, and re-layouts: 126 us -> 19.6 us
  other arithmetic: 143 us -> 36.8 us
  starting transfers between devices: 47.8 us -> 3.68 us
  waiting for transfers between devices: 489 us -> 454 us
    psum x1 -> x8, blocking collectives: 2.47 us -> 557 us  [the longest x7 520 us: on(): return lax.psum(jnp.where(here, v, jnp.zeros_like(v)), ('section', 'pair'))]
    psum x1 -> x7, waiting for transfers between devices: 18.4 us -> 446 us  [the longest x5 286 us: on(): return lax.psum(jnp.where(here, v, jnp.zeros_like(v)), ('section', 'pair'))]
    ppermute x12 -> x2, waiting for transfers between devices: 302 us -> 8.32 us  [the longest x1 5.52 us: body(): g_thid_up = lax.ppermute(g_thid, 'pair', [(2, 0), (3, 1)])]
    another operation x14 -> x0, loops' own time: 187 us -> none  [the longest x7 145 us: body(): lax.switch(branch, backward_table, saved[:rows], saved[rows:], lengths[sl...]
    all_gather x0 -> x5, blocking collectives: none -> 182 us  [the longest x1 41.8 us: body(): dec_rows = lax.all_gather(dec_x, ALL, tiled=True)]
    pallas_call x0 -> x2, Pallas kernels: none -> 179 us  [the longest x1 93 us: reduce(): pl.pallas_call(reduce_kernel, out_shape=jax.ShapeDtypeStruct((2, D, D), b...]
    all_gather x1 -> x0, waiting for transfers between devices: 97.2 us -> none  [body(): weight_cols = lax.all_gather(weights[0], 'pair', axis=1, tiled=True)]
    dot_general x84 -> x71, matrix products: 242 us -> 164 us  [the longest x22 51.7 us: tn(): lax.dot_general(a, b, (((0,), (0,)), ((), ())), preferred_element_type=jn...]
  transfers between devices with their start and end apart: 19 -> 9, of which waited for: 17 -> 7; matrix products, arithmetic and copies ran while one was open for 4% -> 7% of each run, Pallas kernels for 0% -> 11%
where the time goes in v1:
time: 1630 us; the launch traced here: 1620 us
  blocking collectives  739 us (45%)
  waiting for transfers between devices  454 us (28%)
  Pallas kernels  179 us (11%)
  matrix products  171 us (10%)
  other arithmetic  36.8 us (2%)
  local copies, waits for them, and re-layouts  19.6 us (1%)
    psum x7, blocking collectives, on(): return lax.psum(jnp.where(here, v, jnp.zeros_like(v)), ('section', 'pair'))  520 us
    psum x5, waiting for transfers between devices, on(): return lax.psum(jnp.where(here, v, jnp.zeros_like(v)), ('section', 'pair'))  286 us
    psum x1, waiting for transfers between devices, body(): lax.psum(jnp.where((s == 3) & (p < 2), nt(g_thid_up, w), 0.0), ('section'...  97.3 us
    pallas_call x1, Pallas kernels, reduce(): pl.pallas_call(reduce_kernel, out_shape=jax.ShapeDtypeStruct((2, D, D), b...  93 us
    pallas_call x1, Pallas kernels, gather(): pl.pallas_call(gather_kernel, out_shape=jax.ShapeDtypeStruct((12, D, D),...  85.8 us
    psum x1, waiting for transfers between devices, body(): lax.psum(jnp.where(downs, nt(tact, w), 0.0), ('section', 'pair'))  62.4 us
    dot_general x22, matrix products, tn(): lax.dot_general(a, b, (((0,), (0,)), ((), ())), preferred_element_type=jn...  51.7 us
    dot_general x22, matrix products, nt(): lax.dot_general(a, b, (((1,), (1,)), ((), ())), preferred_element_type=jn...  48.2 us
  transfers between devices with their start and end apart: 9, of which 7 were waited for; matrix products, arithmetic and copies ran while one was open for 7% of the time, Pallas kernels for 11%

profile of v1, /device:TPU:0, one launch (start us, length us, event | category | flops | bytes accessed | tf_op | source)
XLA Modules:
  0.0 1618.8 jit_solution(15310429517748121340)
XLA Ops:
  7.2 15.0 all_gather.22
  23.0 41.8 %all-gather = f32[32,1,768]{2,1,0:T(1,128)S(1)} all-gather(f32[1,1,768]{2,1,0:T(1,128)S(1)} %fusion.246), channel_id=2, replica_groups=mesh['section'=4,'pair'=4,'dp'=2] {'section','pair','dp'}, dimensions={0}, use_global_device_ids=true | all-gather | bytes 101376 | tf_op jit(solution)/shard_map/all_gather | solution.py:554
  67.2 71.9 %psum.105 = bf16[32,768]{1,0:T(8,128)(2,1)S(1)} all-reduce(bf16[32,768]{1,0:T(8,128)(2,1)S(1)} %fusion.148), channel_id=1, replica_groups=mesh['section'=4,'pair'=4,'dp'=2] {'section','pair'}, use_global_device_ids=true, to_apply=%region_1.2 | all-reduce | flops 24576 | bytes 98304 | tf_op jit(solution)/shard_map/psum | solution.py:507
  141.6 85.8 %gather.1 = bf16[12,768,768]{2,1,0:T(8,128)(2,1)} custom-call(bf16[768,1536]{1,0:T(8,128)(2,1)} %bitcast.326), custom_call_target="tpu_custom_call" | custom-call | tf_op jit(solution)/shard_map/gather/pallas_call | solution.py:235
  231.9 3.0 convolution_convert_fusion.15
  240.4 7.6 fusion.286
  248.1 5.8 fusion.98
  253.9 2.7 fusion.65
  257.3 3.2 fusion.113
  262.6 2.7 fusion.127
  265.3 2.7 fusion.134
  268.1 4.0 fusion.116
  272.1 3.6 fusion.123
  275.7 3.7 fusion.130
  282.8 77.5 %psum.107 = bf16[32,768]{1,0:T(8,128)(2,1)S(1)} all-reduce(bf16[32,768]{1,0:T(8,128)(2,1)S(1)} %fusion.149), channel_id=1, replica_groups=mesh['section'=4,'pair'=4,'dp'=2] {'section','pair'}, use_global_device_ids=true, to_apply=%region_4.5 | all-reduce | flops 24576 | bytes 98304 | tf_op jit(solution)/shard_map/psum | solution.py:507
  362.1 5.8 multiply_reduce_fusion.3
  370.2 98.2 %all-reduce.10.cloned.1.call-done = bf16[32,16,768]{2,1,0:T(8,128)(2,1)} async-done(((bf16[32,16,768]{2,1,0:T(8,128)(2,1)}), bf16[32,16,768]{2,1,0:T(8,128)(2,1)}) %all-reduce.10.cloned.1.call-update) | async-done | bytes 786448 | tf_op jit(solution)/shard_map/psum | solution.py:507
  470.0 41.7 %all-gather.1 = bf16[512,768]{1,0:T(8,128)(2,1)S(1)} all-gather(bf16[16,768]{1,0:T(8,128)(2,1)S(1)} %convolution_convert_fusion.22), channel_id=3, replica_groups=mesh['section'=4,'pair'=4,'dp'=2] {'section','pair','dp'}, dimensions={0}, use_global_device_ids=true | all-gather | bytes 811008 | tf_op jit(solution)/shard_map/all_gather | solution.py:569
  512.7 71.8 %psum.109 = bf16[32,768]{1,0:T(8,128)(2,1)S(1)} all-reduce(bf16[32,768]{1,0:T(8,128)(2,1)S(1)} %convert_select_fusion.3), channel_id=1, replica_groups=mesh['section'=4,'pair'=4,'dp'=2] {'section','pair'}, use_global_device_ids=true, to_apply=%region_14.15 | all-reduce | flops 24576 | bytes 98304 | tf_op jit(solution)/shard_map/psum | solution.py:507
  585.6 73.1 %psum.110 = bf16[32,768]{1,0:T(8,128)(2,1)S(1)} all-reduce(f32[32,768]{1,0:T(8,128)S(1)} %fusion.146), channel_id=1, replica_groups=mesh['section'=4,'pair'=4,'dp'=2] {'section','pair'}, use_global_device_ids=true, to_apply=%region_15.16 | all-reduce | flops 24576 | bytes 147456 | tf_op jit(solution)/shard_map/psum | solution.py:507
  662.7 2.8 collective-permute-done
  667.9 41.7 %all-gather.2 = f32[32,1,768]{2,1,0:T(1,128)S(1)} all-gather(f32[1,1,768]{2,1,0:T(1,128)S(1)} %fusion.251), channel_id=4, replica_groups=mesh['section'=4,'pair'=4,'dp'=2] {'section','pair','dp'}, dimensions={0}, use_global_device_ids=true | all-gather | bytes 101376 | tf_op jit(solution)/shard_map/all_gather | solution.py:555
  709.6 62.4 %all-reduce.12.cloned.1.call-done = f32[32,768]{1,0:T(8,128)} async-done(((f32[32,768]{1,0:T(8,128)}), f32[32,768]{1,0:T(8,128)}) %all-reduce.12.cloned.1.call-update) | async-done | bytes 98320 | tf_op jit(solution)/shard_map/psum | solution.py:580
  778.7 5.5 collective-permute-done.1
  791.8 97.3 %all-reduce.14.cloned.1.call-done = f32[32,768]{1,0:T(8,128)} async-done(((f32[32,768]{1,0:T(8,128)}), f32[32,768]{1,0:T(8,128)}) %all-reduce.14.cloned.1.call-update) | async-done | bytes 98320 | tf_op jit(solution)/shard_map/psum | solution.py:586
  893.2 77.2 %psum.113 = bf16[32,768]{1,0:T(8,128)(2,1)} all-reduce(bf16[32,768]{1,0:T(8,128)(2,1)} %fusion.150), channel_id=1, replica_groups=mesh['section'=4,'pair'=4,'dp'=2] {'section','pair'}, use_global_device_ids=true, to_apply=%region_22.23 | all-reduce | flops 24576 | bytes 98304 | tf_op jit(solution)/shard_map/psum | solution.py:507
  974.3 3.9 fusion.223
  980.7 98.6 %all-reduce.16.cloned.1.call-done = bf16[32,16,768]{2,1,0:T(8,128)(2,1)} async-done(((bf16[32,16,768]{2,1,0:T(8,128)(2,1)}), bf16[32,16,768]{2,1,0:T(8,128)(2,1)}) %all-reduce.16.cloned.1.call-update) | async-done | bytes 786448 | tf_op jit(solution)/shard_map/psum | solution.py:507
  1085.2 3.3 fusion.64
  1088.5 3.0 fusion.59
  1105.2 7.0 fusion.101
  1112.3 9.2 multiply_reduce_fusion
  1121.5 6.9 multiply_convert_fusion
  1138.3 4.2 fusion.34
  1143.1 41.7 %all-gather.3 = bf16[512,768]{1,0:T(8,128)(2,1)S(1)} all-gather(bf16[16,768]{1,0:T(8,128)(2,1)S(1)} %fusion.152), channel_id=5, replica_groups=mesh['section'=4,'pair'=4,'dp'=2] {'section','pair','dp'}, dimensions={0}, use_global_device_ids=true | all-gather | bytes 811008 | tf_op jit(solution)/shard_map/all_gather | solution.py:597
  1185.7 72.1 %psum.115 = bf16[32,768]{1,0:T(8,128)(2,1)S(1)} all-reduce(bf16[32,768]{1,0:T(8,128)(2,1)S(1)} %convert_select_fusion.2), channel_id=1, replica_groups=mesh['section'=4,'pair'=4,'dp'=2] {'section','pair'}, use_global_device_ids=true, to_apply=%region_30.31 | all-reduce | flops 24576 | bytes 98304 | tf_op jit(solution)/shard_map/psum | solution.py:507
  1259.0 3.5 fusion.77
  1262.5 3.2 fusion.79
  1283.4 93.0 %reduce.15 = bf16[2,768,768]{2,1,0:T(8,128)(2,1)} custom-call(bf16[12,768,768]{2,1,0:T(8,128)(2,1)} %fusion.97.g_ref), custom_call_target="tpu_custom_call" | custom-call | tf_op jit(solution)/shard_map/reduce/pallas_call | solution.py:443
  1376.4 3.2 slice_bitcast_fusion.1
  1379.7 37.0 %psum.119 = f32[2,2,768]{2,1,0:T(2,128)} all-reduce(f32[2,2,768]{2,1,0:T(2,128)S(1)} %reshape.475), channel_id=1, replica_groups=mesh['section'=4,'pair'=4,'dp'=2] {'section','pair','dp'}, use_global_device_ids=true, to_apply=%region_39.40 | all-reduce | flops 3072 | bytes 24576 | tf_op jit(solution)/shard_map/psum | solution.py:642
  1416.8 3.0 fusion.180
  1424.6 2.7 fusion.219
  1427.3 76.0 %psum.117 = bf16[32,768]{1,0:T(8,128)(2,1)S(1)} all-reduce(bf16[32,768]{1,0:T(8,128)(2,1)S(1)} %fusion.151), channel_id=1, replica_groups=mesh['section'=4,'pair'=4,'dp'=2] {'section','pair'}, use_global_device_ids=true, to_apply=%region_33.34 | all-reduce | flops 24576 | bytes 98304 | tf_op jit(solution)/shard_map/psum | solution.py:507
  1506.5 3.0 select_select_fusion
  1512.4 4.2 fusion.6
  1516.6 89.1 %all-reduce.20.cloned.1.call-done = f32[32,768]{1,0:T(8,128)} async-done(((f32[32,768]{1,0:T(8,128)}), f32[32,768]{1,0:T(8,128)}) %all-reduce.20.cloned.1.call-update) | async-done | bytes 98320 | tf_op jit(solution)/shard_map/psum | solution.py:507
  1608.2 3.3 fusion.254
  (364 shorter events, 123.2 us)
Async XLA Ops:
  7.2 230.1 %copy-start = (s32[4,1]{0,1:T(1,128)S(1)}, s32[4,1]{0,1:T(1,128)}, u32[]{:S(2)}) copy-start(s32[4,1]{0,1:T(1,128)} %param.8) | copy-start | bytes 52
  7.2 272.2 %all-reduce.8.cloned.1.call-start = ((), (), s32[]{:S(2)}) async-start(), calls=%async_computation | async-start | bytes 196608 | tf_op jit(solution)/shard_map/psum | solution.py:507
  22.3 119.2 %copy-start.49 = (f32[768]{0:T(1024)}, f32[768]{0:T(1024)S(1)}, u32[]{:S(2)}) copy-start(f32[768]{0:T(1024)S(1)} %get-tuple-element.25) | copy-start | bytes 9220
  22.3 212.6 %copy-start.53 = (f32[768]{0:T(1024)}, f32[768]{0:T(1024)S(1)}, u32[]{:S(2)}) copy-start(f32[768]{0:T(1024)S(1)} %get-tuple-element.23) | copy-start | bytes 9220
  22.3 243.0 %copy-start.51 = (f32[768]{0:T(1024)}, f32[768]{0:T(1024)S(1)}, u32[]{:S(2)}) copy-start(f32[768]{0:T(1024)S(1)} %get-tuple-element.22) | copy-start | bytes 9220
  65.5 161.9 %copy-start.84 = (f32[32]{0:T(128)}, f32[32]{0:T(128)S(1)}, u32[]{:S(2)}) copy-start(f32[32]{0:T(128)S(1)} %get-tuple-element.39) | copy-start | bytes 388
  139.1 88.3 %copy-start.43 = (bf16[32,768]{1,0:T(8,128)(2,1)}, bf16[32,768]{1,0:T(8,128)(2,1)S(1)}, u32[]{:S(2)}) copy-start(bf16[32,768]{1,0:T(8,128)(2,1)S(1)} %psum.105) | copy-start | bytes 147460
  141.6 326.8 %all-reduce.10.cloned.1.call-start = ((), (), s32[]{:S(2)}) async-start(), calls=%async_computation.1 | async-start | bytes 1572864 | tf_op jit(solution)/shard_map/psum | solution.py:507
  237.3 10.7 copy-start.32
  240.1 8.0 copy-start.20
  240.4 7.7 copy-start.10
  256.6 105.5 %copy-start.7 = (bf16[512,768]{1,0:T(8,128)(2,1)}, bf16[512,768]{1,0:T(8,128)(2,1)S(1)}, u32[]{:S(2)}) copy-start(bf16[512,768]{1,0:T(8,128)(2,1)S(1)} %get-tuple-element.49) | copy-start | bytes 2359300
  257.3 8.1 copy-start.61
  268.0 7.7 copy-start.102
  362.1 410.0 %all-reduce.12.cloned.1.call-start = ((), (), s32[]{:S(2)}) async-start(), calls=%async_computation.2 | async-start | bytes 196608 | tf_op jit(solution)/shard_map/psum | solution.py:580
  368.6 143.2 %copy-start.47 = (f32[16,768]{1,0:T(8,128)}, f32[16,768]{1,0:T(8,128)S(1)}, u32[]{:S(2)}) copy-start(f32[16,768]{1,0:T(8,128)S(1)} %broadcast_select_fusion.2) | copy-start | bytes 147460
  469.5 42.2 %copy-start.57 = (f32[16]{0:T(128)}, f32[16]{0:T(128)S(1)}, u32[]{:S(2)}) copy-start(f32[16]{0:T(128)S(1)} %get-tuple-element.52) | copy-start | bytes 196
  469.7 42.0 %copy-start.59 = (f32[16]{0:T(128)}, f32[16]{0:T(128)S(1)}, u32[]{:S(2)}) copy-start(f32[16]{0:T(128)S(1)} %fusion.212) | copy-start | bytes 196
  511.8 73.4 %copy-start.22 = (f32[32,768]{1,0:T(8,128)S(1)}, f32[32,768]{1,0:T(8,128)}, u32[]{:S(2)}) copy-start(f32[32,768]{1,0:T(8,128)} %all-reduce.8.cloned.1.call-done) | copy-start | bytes 294916
  659.3 8.5 copy-start.82
  660.5 7.3 copy-start.86
  660.5 4.9 collective-permute-start
  667.8 221.2 %all-reduce.14.cloned.1.call-start = ((), (), s32[]{:S(2)}) async-start(), calls=%async_computation.3 | async-start | bytes 196608 | tf_op jit(solution)/shard_map/psum | solution.py:586
  709.6 63.5 %copy-start.29 = (f32[32,1,768]{2,1,0:T(1,128)}, f32[32,1,768]{2,1,0:T(1,128)S(1)}, u32[]{:S(2)}) copy-start(f32[32,1,768]{2,1,0:T(1,128)S(1)} %all-gather.2) | copy-start | bytes 294916
  777.5 6.8 collective-permute-start.1
  786.6 292.7 %all-reduce.16.cloned.1.call-start = ((), (), s32[]{:S(2)}) async-start(), calls=%async_computation.4 | async-start | bytes 1572864 | tf_op jit(solution)/shard_map/psum | solution.py:507
  972.9 449.2 %all-reduce.18.cloned.1.call-start = ((), (), s32[]{:S(2)}) async-start(), calls=%async_computation.5 | async-start | bytes 196608 | tf_op jit(solution)/shard_map/psum | solution.py:507
  978.3 101.1 %copy-start.58 = (f32[16]{0:T(128)S(1)}, f32[16]{0:T(128)}, u32[]{:S(2)}) copy-start(f32[16]{0:T(128)} %copy-done.57) | copy-start | bytes 196
  978.3 101.1 %copy-start.60 = (f32[16]{0:T(128)S(1)}, f32[16]{0:T(128)}, u32[]{:S(2)}) copy-start(f32[16]{0:T(128)} %copy-done.59) | copy-start | bytes 196
  1079.3 12.1 slice-start
  1085.1 7.8 copy-start.35
  1088.5 8.7 copy-start.30
  1105.2 7.0 copy-start.33
  1105.2 7.0 copy-start.34
  1105.2 16.3 %slice-start.4 = ((s8[12582912]{0:T(1024)(128)(4,1)}), s8[4194304]{0:T(1024)(128)(4,1)S(1)}, s32[]{:S(2)}) async-start(s8[12582912]{0:T(1024)(128)(4,1)} %bitcast.339), calls=%async_computation.11 | async-start | bytes 8388608
  1105.2 16.3 %slice-start.5 = ((s8[12582912]{0:T(1024)(128)(4,1)}), s8[4194304]{0:T(1024)(128)(4,1)S(1)}, s32[]{:S(2)}) async-start(s8[12582912]{0:T(1024)(128)(4,1)} %bitcast.339), calls=%async_computation.12 | async-start | bytes 8388608
  1112.2 26.1 %copy-start.37 = (bf16[12,64,512]{2,1,0:T(8,128)(2,1)}, bf16[12,64,512]{2,1,0:T(8,128)(2,1)S(1)}, u32[]{:S(2)}) copy-start(bf16[12,64,512]{2,1,0:T(8,128)(2,1)S(1)} %fusion.101) | copy-start | bytes 2359300
  1112.3 9.2 slice-start.6
  1138.3 46.5 %copy-start.48 = (f32[16,768]{1,0:T(8,128)S(1)}, f32[16,768]{1,0:T(8,128)}, u32[]{:S(2)}) copy-start(f32[16,768]{1,0:T(8,128)} %copy-done.47) | copy-start | bytes 147460
  1258.9 346.8 %all-reduce.20.cloned.1.call-start = ((), (), s32[]{:S(2)}) async-start(), calls=%async_computation.6 | async-start | bytes 196608 | tf_op jit(solution)/shard_map/psum | solution.py:507
  1376.4 40.4 %copy-start.74 = (f32[512]{0:T(512)S(1)}, f32[512]{0:T(512)}, u32[]{:S(2)}) copy-start(f32[512]{0:T(512)} %get-tuple-element.32) | copy-start | bytes 6148
  1376.4 40.4 %copy-start.76 = (f32[512]{0:T(512)S(1)}, f32[512]{0:T(512)}, u32[]{:S(2)}) copy-start(f32[512]{0:T(512)} %broadcast_multiply_fusion.2) | copy-start | bytes 6148
  1424.6 79.9 %copy-start.50 = (f32[768]{0:T(1024)S(1)}, f32[768]{0:T(1024)}, u32[]{:S(2)}) copy-start(f32[768]{0:T(1024)} %copy-done.49) | copy-start | bytes 9220
  1424.6 79.9 %copy-start.85 = (f32[32]{0:T(128)S(1)}, f32[32]{0:T(128)}, u32[]{:S(2)}) copy-start(f32[32]{0:T(128)} %copy-done.84) | copy-start | bytes 388
  1512.3 95.1 %copy-start.72 = (f32[1,768]{1,0:T(1,128)S(1)}, f32[1,768]{1,0:T(1,128)}, u32[]{:S(2)}) copy-start(f32[1,768]{1,0:T(1,128)} %stack.98) | copy-start | bytes 9220
  1512.3 95.1 %copy-start.73 = (f32[1,768]{1,0:T(1,128)S(1)}, f32[1,768]{1,0:T(1,128)}, u32[]{:S(2)}) copy-start(f32[1,768]{1,0:T(1,128)} %stack.97) | copy-start | bytes 9220
  1512.4 95.1 %copy-start.46 = (f32[2,2,768]{2,1,0:T(2,128)S(1)}, f32[2,2,768]{2,1,0:T(2,128)}, u32[]{:S(2)}) copy-start(f32[2,2,768]{2,1,0:T(2,128)} %psum.119) | copy-start | bytes 36868
  1512.4 99.1 %copy-start.1 = (s32[4,1]{0,1:T(1,128)S(1)}, s32[4,1]{0,1:T(1,128)}, u32[]{:S(2)}) copy-start(s32[4,1]{0,1:T(1,128)} %param.8) | copy-start | bytes 52
  (75 other events, 206.6 us)
Sparse Core Ops, SparseCore 0:
  141.7 99.6 all-reduce.7
  362.2 106.1 all-reduce.9
  667.9 104.0 all-reduce.11
  786.7 102.2 all-reduce.13
  973.1 106.2 all-reduce.15
  1259.0 99.7 all-reduce.17
  1506.6 98.9 all-reduce.19
